TPU v7x, 256 devices: a whole 4x4x8 slice. The times are simulated.
256 devices in a mesh: group: 8 (over x_lo, y), fsdp: 32 (over x_hi, z, core).
Axes of the slice: x: 4 (x_hi: 2, x_lo: 2; x = x_hi * 2 + x_lo), y: 4, z: 8, core: 2. Of those that a mesh axis runs over, the one named last changes fastest.
Arguments:
- delta_codes: int32 [8, 8192, 512], P('group', 'fsdp'), may hold values from -32704 to 32704
- master_weights: float32 [8192, 512], P('fsdp'), may hold values from -6 to 6
- outer_momentum: float32 [8192, 512], P('fsdp'), may hold values from -3 to 3
- activations: bfloat16 [65536, 8192], P(('group', 'fsdp')), may hold values from -6 to 6
- key_cotangent: bfloat16 [65536, 512], P(('group', 'fsdp')), may hold values from -6 to 6
Outputs:
- new_weights: float32 [8192, 512], P('fsdp')
- new_momentum: float32 [8192, 512], P('fsdp')
- projected_keys: bfloat16 [65536, 512], P(('group', 'fsdp'))
- input_grads: bfloat16 [65536, 8192], P(('group', 'fsdp'))
- weight_grads: float32 [8, 8192, 512], P('group', 'fsdp')
All inputs are finite; a program needn't handle non-finite values.
Results may differ from a plain program's by a relative error of at most 0.007.
Values may be sent and summed in bfloat16 or wider, within the bound.
A program may use at most 128 MiB of HBM per device.

v0:
```python
import jax
import jax.numpy as jnp
from jax import lax
from jax.sharding import PartitionSpec as P

unit_step = 1.0 / 4096.0


def dequantize(delta_codes):
    blocks = delta_codes.reshape(delta_codes.shape[:-1] + (delta_codes.shape[-1] // 128, 128))
    largest = jnp.max(jnp.abs(blocks), axis=-1, keepdims=True)
    block_scale = largest // 127 + 1
    magnitude = (jnp.abs(blocks) + block_scale // 2) // block_scale
    quantized = jnp.sign(blocks) * magnitude
    values = (quantized * block_scale).astype(jnp.float32) * unit_step
    return values.reshape(delta_codes.shape)


def nesterov(weights, momentum, total, groups):
    outer_grad = total / groups
    moved = 0.9 * momentum + outer_grad
    return (weights - 0.7 * (outer_grad + 0.9 * moved), moved)


def body(delta_codes, master_weights, outer_momentum, activations, key_cotangent):
    groups = lax.axis_size("group")
    dequantized = dequantize(delta_codes)[0]
    total = lax.psum(dequantized.astype(jnp.bfloat16), "group").astype(jnp.float32)
    new_weights, new_momentum = nesterov(master_weights, outer_momentum, total, groups)
    inner_weights = new_weights.astype(jnp.bfloat16)
    width = activations.shape[1]
    scale = width ** (-0.5)
    piece = lax.all_gather(inner_weights, "fsdp", axis=0, tiled=True)
    features = activations
    keys_sum = jnp.dot(features, piece, preferred_element_type=jnp.float32)
    back = lax.dot_general(
        key_cotangent, piece, (((1,), (1,)), ((), ())), preferred_element_type=jnp.float32
    )
    input_sum = back
    keys_sum, input_sum = (keys_sum, input_sum)
    projected_keys = (keys_sum * scale).astype(jnp.bfloat16)
    input_grads = (input_sum * scale).astype(jnp.bfloat16)
    features = activations
    weight_grads = lax.psum_scatter(
        lax.dot_general(
            features, key_cotangent, (((0,), (0,)), ((), ())), preferred_element_type=jnp.float32
        )
        * scale,
        "fsdp",
        scatter_dimension=0,
        tiled=True,
    )
    return (new_weights, new_momentum, projected_keys, input_grads, weight_grads[None])


def solution(mesh):
    placed = (
        P("group", "fsdp", None),
        P("fsdp", None),
        P("fsdp", None),
        P(("group", "fsdp"), None),
        P(("group", "fsdp"), None),
    )
    return jax.shard_map(
        body,
        mesh=mesh,
        in_specs=placed,
        out_specs=(
            P("fsdp", None),
            P("fsdp", None),
            P(("group", "fsdp"), None),
            P(("group", "fsdp"), None),
            P("group", "fsdp", None),
        ),
        check_vma=False,
    )
```

profile of v0, /device:TPU:1, one launch (start us, length us, event | category | flops | bytes accessed | tf_op | source)
XLA Modules:
  0.0 434.1 jit_solution(8302694735613577317)
XLA Ops:
  7.2 0.0 copy-start
  7.2 0.0 all-reduce.2.cloned.1.call-start
  7.2 1.1 abs.23
  8.4 0.2 abs.25
  8.6 4.4 %reduce_max.9 = s32[256,4]{1,0:T(8,128)S(1)} reduce(s32[256,4,128]{2,1,0:T(4,128)S(1)} %abs.25, s32[]{:T(128)} %constant.31.clone.1), dimensions={2}, to_apply=%region_0.0 | reduce | flops 130048 | bytes 528388 | tf_op jit(solution)/shard_map/reduce_max | solution.py:11
  13.0 0.2 add_select_fusion.1
  13.2 0.3 rem.58
  13.5 0.3 ne.90
  13.8 0.3 add.61
  14.2 7.2 %fusion.8 = bf16[256,512]{1,0:T(8,128)(2,1)} fusion(s32[1,256,512]{2,1,0:T(8,128)} %param.5, s32[32,8,4,128]{3,2,1,0:T(4,128)S(1)} %bitcast.41, s32[32,8,4,128]{3,2,1,0:T(4,128)S(1)} %bitcast.42, s32[32,8,4,128]{3,2,1,0:T(4,128)S(1)} %bitcast.40), kind=kLoop, calls=%fused_computation.12 | loop fusion | flops 2097152 | bytes 2359296 | tf_op jit(solution)/shard_map/convert_element_type | solution.py:28
  21.3 0.0 all-reduce.2.cloned.1.call-update
  21.4 0.0 all-gather.2.cloned.1.call-start
  21.4 78.0 %all-reduce.2.cloned.1.call-done = bf16[256,512]{1,0:T(8,128)(2,1)} async-done(((bf16[256,512]{1,0:T(8,128)(2,1)}), bf16[256,512]{1,0:T(8,128)(2,1)}) %all-reduce.2.cloned.1.call-update) | async-done | bytes 262160 | tf_op jit(solution)/shard_map/psum | solution.py:28
  99.4 2.5 fusion.15
  101.9 0.0 all-gather.2.cloned.1.call-update
  101.9 0.2 reduce-scatter.2.cloned.1.call-start
  102.2 0.0 copy-done
  102.2 10.3 %convolution_multiply_fusion = f32[8192,512]{1,0:T(8,128)} fusion(bf16[256,8192]{1,0:T(8,128)(2,1)} %param.8, bf16[256,512]{1,0:T(8,128)(2,1)S(1)} %copy-done), kind=kOutput, calls=%fused_computation | convolution fusion | flops 2151677952 | bytes 21233664 | tf_op jit(solution)/shard_map/dot_general | solution.py:45
  112.5 0.0 reduce-scatter.2.cloned.1.call-update
  112.5 97.0 %all-gather.2.cloned.1.call-done = bf16[8192,512]{1,0:T(8,128)(2,1)} async-done(((bf16[256,512]{1,0:T(8,128)(2,1)}), bf16[8192,512]{1,0:T(8,128)(2,1)}) %all-gather.2.cloned.1.call-update) | async-done | bytes 8388624 | tf_op jit(solution)/shard_map/all_gather | solution.py:33
  209.5 7.7 %fusion.1 = bf16[256,8192]{0,1:T(8,128)(2,1)} fusion(bf16[8192,512]{1,0:T(8,128)(2,1)} %all-gather.2.cloned.1.call-done, bf16[256,512]{1,0:T(8,128)(2,1)S(1)} %copy-done), kind=kOutput, calls=%fused_computation.3 | convolution fusion | flops 2151677952 | bytes 12845056 | tf_op jit(solution)/shard_map/dot_general | solution.py:36
  217.2 6.3 %copy.11 = bf16[256,8192]{1,0:T(8,128)(2,1)} copy(bf16[256,8192]{0,1:T(8,128)(2,1)} %fusion.1) | data formatting | bytes 8388608
  223.6 8.1 %fusion.3 = bf16[256,512]{0,1:T(8,128)(2,1)S(1)} fusion(bf16[8192,512]{1,0:T(8,128)(2,1)} %all-gather.2.cloned.1.call-done, bf16[256,8192]{1,0:T(8,128)(2,1)} %param.8), kind=kOutput, calls=%fused_computation.6 | convolution fusion | flops 2147745792 | bytes 12845056 | tf_op jit(solution)/shard_map/dot_general | solution.py:35
  231.7 0.8 copy.10
  232.5 195.1 %reduce-scatter.2.cloned.1.call-done = f32[256,512]{1,0:T(8,128)} async-done(((f32[8192,512]{1,0:T(8,128)}), f32[256,512]{1,0:T(8,128)}) %reduce-scatter.2.cloned.1.call-update) | async-done | bytes 524304 | tf_op jit(solution)/shard_map/reduce_scatter | solution.py:44
  (1 shorter events, 0.0 us)
Async XLA Ops:
  7.2 95.0 %copy-start = (bf16[256,512]{1,0:T(8,128)(2,1)S(1)}, bf16[256,512]{1,0:T(8,128)(2,1)}, u32[]{:S(2)}) copy-start(bf16[256,512]{1,0:T(8,128)(2,1)} %param.9) | copy-start | bytes 786436
  7.2 92.2 %all-reduce.2.cloned.1.call-start = ((), (), s32[]{:S(2)}) async-start(), calls=%async_computation.1 | async-start | bytes 524288 | tf_op jit(solution)/shard_map/psum | solution.py:28
  21.4 188.2 %all-gather.2.cloned.1.call-start = ((), (), s32[]{:S(2)}) async-start(), calls=%async_computation.2 | async-start | bytes 8650752 | tf_op jit(solution)/shard_map/all_gather | solution.py:33
  101.9 325.7 %reduce-scatter.2.cloned.1.call-start = ((), (), s32[]{:S(2)}) async-start(), calls=%async_computation.3 | async-start | bytes 17301504 | tf_op jit(solution)/shard_map/reduce_scatter | solution.py:44
Sparse Core Ops, SparseCore 0:
  21.5 77.8 all-reduce.1
  103.1 106.3 all-gather.1
  215.4 212.2 reduce-scatter.1
where the time goes:
time: 438 us; the launch traced here: 434 us
  waiting for transfers between devices  370 us (84%)
  matrix products  26.1 us (6%)
  other arithmetic  15.4 us (4%)
  between operations  13.8 us (3%)
  local copies, waits for them, and re-layouts  8.37 us (2%)
    reduce_scatter x1, waiting for transfers between devices, body(): lax.psum_scatter(lax.dot_general(features, key_cotangent, (((0,), (0,)),...  195 us
    all_gather x1, waiting for transfers between devices, body(): piece = lax.all_gather(inner_weights, 'fsdp', axis=0, tiled=True)  97 us
    psum x1, waiting for transfers between devices, body(): lax.psum(dequantized.astype(jnp.bfloat16), 'group').astype(jnp.float32)  78 us
    dot_general x1, matrix products, body(): lax.dot_general(features, key_cotangent, (((0,), (0,)), ((), ())), prefer...  10.3 us
  transfers between devices with their start and end apart: 3, of which 3 were waited for; matrix products, arithmetic and copies ran while one was open for 8% of the time, Pallas kernels for 0%

commit v1 on v0

v1 whole, which is shorter than its diff:
```python
import functools

import jax
import jax.numpy as jnp
from jax import lax
from jax.experimental import pallas as pl
from jax.experimental.pallas import tpu as pltpu
from jax.sharding import PartitionSpec as P

MESH = pl.DeviceIdType.MESH
F32 = jnp.float32
BF16 = jnp.bfloat16
NX, NY, NZ = 4, 4, 8
GROUPS = 8


def device(x, y, z, c):
    return (lax.rem(x, 2) * 4 + y, lax.div(x, 2) * 16 + z * 2 + c)


def up(v, d, n):
    return lax.rem(v + d, n)


def dequantize(codes):
    values = codes.astype(F32)
    size = jnp.abs(values)
    largest = jnp.max(size, axis=-1, keepdims=True)
    scale = jnp.floor((largest + 0.5) / 127.0) + 1.0
    half = jnp.floor(scale * 0.5)
    magnitude = jnp.floor((size + half + 0.5) / scale)
    signed = jnp.where(values < 0.0, -magnitude, magnitude)
    return signed * scale * (1.0 / 4096.0)


def nesterov(total, weights, momentum):
    outer_grad = total.astype(F32) / GROUPS
    moved = 0.9 * momentum + outer_grad
    return weights - 0.7 * (outer_grad + 0.9 * moved), moved


def kernel(
    delta_hbm, master_hbm, momentum_hbm, acts_hbm, cot_hbm,
    weights_out, moved_out, keys_out, grads_hbm, wgrad_out,
    delta, master, momentum, cot, cot_t, acts,
    coded, coded_in, total, gathered,
    chain_out, chain_in, cross_out, cross_in, cross_own,
    keys, keys_in, back,
    load_sem, acts_load, acts_send, acts_recv, pair_send, pair_recv,
    coded_send, coded_recv, total_send, total_recv,
    z_send, z_recv, x_send, x_recv, y_send, y_recv, f_send, f_recv,
    chain_send, chain_recv, cross_send, cross_recv,
    back_store, back_send, back_recv,
):
    tokens, width = acts_hbm.shape
    kw = cot_hbm.shape[1]
    block = width // 32
    piece = block // GROUPS
    half = kw // 2
    out_scale = width ** (-0.5)

    g, f = lax.axis_index("group"), lax.axis_index("fsdp")
    y, x_lo = lax.rem(g, NY), lax.div(g, NY)
    c, z, x_hi = lax.rem(f, 2), lax.rem(lax.div(f, 2), NZ), lax.div(f, 16)
    x = 2 * x_hi + x_lo
    other = 1 - c
    sibling = device(x, y, z, other)

    def member(j):
        return device(2 * x_hi + lax.div(j, NY), lax.rem(j, NY), z, c)

    def remote(src, dst, send, recv, to):
        return pltpu.make_async_remote_copy(
            src_ref=src, dst_ref=dst, send_sem=send, recv_sem=recv, device_id=to, device_id_type=MESH
        )

    def columns(hi, zz, core):
        return pl.ds(pl.multiple_of((hi * 16 + zz * 2 + core) * block, block), block)

    def tokens_of(core):
        return pl.ds(pl.multiple_of(core * tokens, tokens), tokens)

    loads = [
        pltpu.make_async_copy(delta_hbm, delta, load_sem.at[0]),
        pltpu.make_async_copy(cot_hbm, cot.at[tokens_of(c)], load_sem.at[1]),
        pltpu.make_async_copy(master_hbm, master, load_sem.at[2]),
        pltpu.make_async_copy(momentum_hbm, momentum, load_sem.at[3]),
    ]
    for load in loads:
        load.start()

    def act_load(zz, hi):
        return pltpu.make_async_copy(
            acts_hbm.at[:, columns(hi, zz, c)], acts.at[zz, hi, tokens_of(c)], acts_load.at[zz, hi]
        )

    def act_swap(zz, hi):
        return remote(
            acts_hbm.at[:, columns(hi, zz, other)], acts.at[zz, hi, tokens_of(c)],
            acts_send.at[zz, hi], acts_recv.at[zz, hi], sibling,
        )

    def act_arrived(zz, hi):
        return remote(
            acts_hbm.at[:, columns(hi, zz, other)], acts.at[zz, hi, tokens_of(other)],
            acts_send.at[zz, hi], acts_recv.at[zz, hi], sibling,
        )

    def far(i):
        step = lax.div(i + 1, 2)
        return lax.rem(z + 4 + step * (2 * lax.rem(i, 2) - 1) * -1 + NZ, NZ)

    @pl.loop(0, NZ)
    def _(i):
        for hi in range(2):
            act_load(far(i), hi).start()

    partners = [sibling]
    partners += [device(x, y, up(z, d, NZ), c) for d in range(1, NZ)]
    partners += [device(up(x, d, NX), y, z, c) for d in range(1, NX)]
    partners += [device(x, up(y, d, NY), z, c) for d in range(1, NY)]
    partners += [device(2 * x_hi + 1 - x_lo, up(y, d, NY), z, c) for d in range(1, NY)]
    barrier = pltpu.get_barrier_semaphore()
    for partner in partners:
        pl.semaphore_signal(barrier, inc=1, device_id=partner, device_id_type=MESH)
    pl.semaphore_wait(barrier, len(partners))

    cot_swap = remote(cot_hbm, cot.at[tokens_of(c)], pair_send.at[0], pair_recv.at[0], sibling)
    cot_swap.start()

    @pl.loop(0, NZ)
    def _(i):
        for hi in range(2):
            act_swap(far(i), hi).start()

    loads[0].wait()
    for j in range(GROUPS):
        for k in range(kw // 128):
            codes = delta[pl.ds(j * piece, piece), pl.ds(k * 128, 128)]
            coded[j, :, pl.ds(k * 128, 128)] = dequantize(codes).astype(BF16)

    def coded_copy(d):
        j = up(g, d, GROUPS)
        return remote(coded.at[j], coded_in.at[g], coded_send.at[d], coded_recv.at[g], member(j))

    def coded_arrived(j):
        return remote(coded.at[j], coded_in.at[j], coded_send.at[0], coded_recv.at[j], sibling)

    @pl.loop(1, GROUPS)
    def _(d):
        coded_copy(d).start()

    loads[1].wait()
    remote(cot_hbm, cot.at[tokens_of(other)], pair_send.at[0], pair_recv.at[0], sibling).wait_recv()
    cot_t[...] = cot[...].T.reshape(2, half, 2 * tokens)

    def acts_ready(zz):
        for hi in range(2):
            act_load(zz, hi).wait()
            act_arrived(zz, hi).wait_recv()

    def chain_copy(way, k):
        to = device(x, y, up(z, 1 if way == 0 else NZ - 1, NZ), c)
        return remote(
            chain_out.at[way, k], chain_in.at[way, k], chain_send.at[way, k], chain_recv.at[way, k], to
        )

    def share(h, zz, hi):
        return jnp.dot(cot_t[h], acts[zz, hi], preferred_element_type=F32)

    def chain(k, first):
        s = lax.div(k + 1, 2)
        for way in range(2):
            zz = up(z, 4 - s if way == 0 else 4 + s, NZ)
            h = lax.rem(k + way, 2)
            if not first:
                chain_copy(way, k - 2).wait_recv()
            for hi in range(2):
                sent = share(h, zz, hi)
                if not first:
                    sent += chain_in[way, k - 2, hi].astype(F32)
                chain_out[way, k, hi] = sent.astype(BF16)
            chain_copy(way, k).start()

    acts_ready(far(0))
    chain(0, True)

    rows = pl.ds(pl.multiple_of(g * piece, piece), piece)

    @pl.loop(1, GROUPS)
    def _(d):
        coded_arrived(up(g, d, GROUPS)).wait_recv()

    summed = coded[g].astype(F32)
    for d in range(1, GROUPS):
        summed += coded_in[up(g, d, GROUPS)].astype(F32)
    total[g] = summed.astype(BF16)
    loads[2].wait()
    loads[3].wait()
    updated, _ = nesterov(total[g], master[rows, :], momentum[rows, :])
    gathered[z, y, x] = updated.astype(BF16)

    def z_copy(d):
        return remote(
            gathered.at[z, y, x], gathered.at[z, y, x], z_send.at[d], z_recv.at[z],
            device(x, y, up(z, d, NZ), c),
        )

    def z_arrived(zz):
        return remote(gathered.at[zz, y, x], gathered.at[zz, y, x], z_send.at[0], z_recv.at[zz], sibling)

    def x_copy(zz, d):
        return remote(
            gathered.at[zz, y, x], gathered.at[zz, y, x], x_send.at[zz, d], x_recv.at[zz, x],
            device(up(x, d, NX), y, z, c),
        )

    def x_arrived(zz, xx):
        return remote(
            gathered.at[zz, y, xx], gathered.at[zz, y, xx], x_send.at[zz, 0], x_recv.at[zz, xx], sibling
        )

    def y_copy(zz, way):
        to = device(x, up(y, 1 if way == 0 else NY - 1, NY), z, c)
        return remote(gathered.at[zz, y], gathered.at[zz, y], y_send.at[zz, way], y_recv.at[zz, way], to)

    def y_arrived(zz, way):
        yy = up(y, NY - 1 if way == 0 else 1, NY)
        return remote(
            gathered.at[zz, yy], gathered.at[zz, yy], y_send.at[zz, way], y_recv.at[zz, way], sibling
        )

    def f_copy(zz, way):
        yy = up(y, NY - 1 if way == 0 else 1, NY)
        to = device(x, up(y, 1 if way == 0 else NY - 1, NY), z, c)
        part = gathered.at[zz, yy, pl.ds(way * 2, 2)]
        return remote(part, part, f_send.at[zz, way], f_recv.at[zz, way], to)

    def f_arrived(zz, way):
        part = gathered.at[zz, up(y, 2, NY), pl.ds(way * 2, 2)]
        return remote(part, part, f_send.at[zz, way], f_recv.at[zz, way], sibling)

    for d in (1, 7, 2, 6, 3, 5, 4):
        z_copy(d).start()
    for d in range(1, NX):
        x_copy(z, d).start()

    def total_copy(d):
        return remote(
            total.at[g], total.at[g], total_send.at[d], total_recv.at[g], member(up(g, d, GROUPS))
        )

    def total_arrived(j):
        return remote(total.at[j], total.at[j], total_send.at[0], total_recv.at[j], sibling)

    @pl.loop(1, GROUPS)
    def _(d):
        total_copy(d).start()

    acts_ready(far(1))
    acts_ready(far(2))
    chain(1, True)

    @pl.loop(3, NZ)
    def _(i):
        acts_ready(far(i))

    def wave(i):
        return lax.rem(z + lax.div(i + 1, 2) * (2 * lax.rem(i, 2) - 1) + NZ, NZ)

    keys[...] = jnp.zeros_like(keys)

    def back_local(zz, hi):
        return pltpu.make_async_copy(
            back.at[zz, hi, tokens_of(c)], grads_hbm.at[:, columns(hi, zz, c)], back_store.at[zz, hi]
        )

    def back_copy(zz, hi):
        return remote(
            back.at[zz, hi, tokens_of(other)], grads_hbm.at[:, columns(hi, zz, c)],
            back_send.at[zz, hi], back_recv.at[zz, hi], sibling,
        )

    def back_arrived(zz, hi):
        return remote(
            back.at[zz, hi, tokens_of(other)], grads_hbm.at[:, columns(hi, zz, other)],
            back_send.at[zz, hi], back_recv.at[zz, hi], sibling,
        )

    def multiply(zz):
        for hi in range(2):
            lower = [gathered[zz, :, 2 * hi + lo].reshape(block // 2, kw) for lo in range(2)]
            w = jnp.concatenate(lower, axis=0)
            grads = lax.dot_general(cot[...], w, (((1,), (1,)), ((), ())), preferred_element_type=F32)
            back[zz, hi] = (grads * out_scale).astype(BF16)
            back_copy(zz, hi).start()
            back_local(zz, hi).start()
            keys[...] += jnp.dot(acts[zz, hi], w, preferred_element_type=F32)

    def cross_copy(h):
        return remote(
            cross_out.at[h], cross_in.at[h], cross_send.at[h], cross_recv.at[h], device(up(x, 2, NX), y, z, c)
        )

    def chain_end():
        for way in range(2):
            for k in (5, 6):
                chain_copy(way, k).wait_recv()
        for mine in range(2):
            hi = x_hi if mine else 1 - x_hi
            for h in range(2):
                done = share(h, z, hi) + chain_in[0, 6 - h, hi].astype(F32) + chain_in[1, 5 + h, hi].astype(F32)
                if mine:
                    cross_own[h] = done
                else:
                    cross_out[h] = done.astype(BF16)
                    cross_copy(h).start()

    @pl.loop(1, NZ + 3)
    def _(i):
        @pl.when(i < NZ)
        def _():
            zz = wave(i)
            z_arrived(zz).wait_recv()
            for d in range(1, NX):
                x_copy(zz, d).start()

        @pl.when(i < NZ + 1)
        def _():
            zz = wave(i - 1)
            for d in range(1, NX):
                x_arrived(zz, up(x, d, NX)).wait_recv()
            for way in range(2):
                y_copy(zz, way).start()

        @pl.when(jnp.logical_and(i >= 2, i < NZ + 2))
        def _():
            zz = wave(i - 2)
            for way in range(2):
                y_arrived(zz, way).wait_recv()
            for way in range(2):
                f_copy(zz, way).start()

        @pl.when(i < 6)
        def _():
            chain(i + 1, False)

        @pl.when(i == 7)
        def _():
            chain_end()

        @pl.when(i >= 3)
        def _():
            zz = wave(i - 3)
            for way in range(2):
                f_arrived(zz, way).wait_recv()
            multiply(zz)

    keys_copy = remote(keys.at[tokens_of(other)], keys_in, pair_send.at[1], pair_recv.at[1], sibling)
    keys_copy.start()

    for j in range(GROUPS):
        @pl.when(g != j)
        def _():
            total_arrived(j).wait_recv()

    for j in range(GROUPS):
        own = pl.ds(j * piece, piece)
        weights_out[own, :], moved_out[own, :] = nesterov(total[j], master[own, :], momentum[own, :])

    for h in range(2):
        cross_copy(h).wait_recv()
        wgrad_out[pl.ds(h * half, half), :] = (cross_own[h] + cross_in[h].astype(F32)) * out_scale

    keys_copy.wait_recv()
    keys_out[...] = ((keys[tokens_of(c), :] + keys_in[...]) * out_scale).astype(BF16)

    cot_swap.wait_send()
    keys_copy.wait_send()
    for h in range(2):
        cross_copy(h).wait_send()

    @pl.loop(0, NZ)
    def _(zz):
        for hi in range(2):
            act_swap(zz, hi).wait_send()
            back_local(zz, hi).wait()
            back_copy(zz, hi).wait_send()
            back_arrived(zz, hi).wait_recv()
        for d in range(1, NX):
            x_copy(zz, d).wait_send()
        for way in range(2):
            y_copy(zz, way).wait_send()
            f_copy(zz, way).wait_send()

    @pl.loop(1, NZ)
    def _(d):
        coded_copy(d).wait_send()
        total_copy(d).wait_send()
        z_copy(d).wait_send()
        for way in range(2):
            chain_copy(way, d - 1).wait_send()


def body(delta_codes, master_weights, outer_momentum, activations, key_cotangent):
    tokens, width = activations.shape
    rows, kw = master_weights.shape
    block, piece, half = width // 32, width // 32 // GROUPS, kw // 2
    dma = pltpu.SemaphoreType.DMA
    hbm = pl.BlockSpec(memory_space=pl.ANY)
    vmem = pl.BlockSpec(memory_space=pltpu.VMEM)
    weights, moved, keys, grads, wgrad = pl.pallas_call(
        kernel,
        name="outer_step",
        out_shape=(
            jax.ShapeDtypeStruct((rows, kw), F32),
            jax.ShapeDtypeStruct((rows, kw), F32),
            jax.ShapeDtypeStruct((tokens, kw), BF16),
            jax.ShapeDtypeStruct((tokens, width), BF16),
            jax.ShapeDtypeStruct((kw, block), F32),
        ),
        in_specs=[hbm] * 5,
        out_specs=(vmem, vmem, vmem, hbm, vmem),
        scratch_shapes=[
            pltpu.VMEM((rows, kw), jnp.int32),
            pltpu.VMEM((rows, kw), F32),
            pltpu.VMEM((rows, kw), F32),
            pltpu.VMEM((2 * tokens, kw), BF16),
            pltpu.VMEM((2, half, 2 * tokens), BF16),
            pltpu.VMEM((NZ, 2, 2 * tokens, block), BF16),
            pltpu.VMEM((GROUPS, piece, kw), BF16),
            pltpu.VMEM((GROUPS, piece, kw), BF16),
            pltpu.VMEM((GROUPS, piece, kw), BF16),
            pltpu.VMEM((NZ, NY, NX, piece, kw), BF16),
            pltpu.VMEM((2, 7, 2, half, block), BF16),
            pltpu.VMEM((2, 7, 2, half, block), BF16),
            pltpu.VMEM((2, half, block), BF16),
            pltpu.VMEM((2, half, block), BF16),
            pltpu.VMEM((2, half, block), F32),
            pltpu.VMEM((2 * tokens, kw), F32),
            pltpu.VMEM((tokens, kw), F32),
            pltpu.VMEM((NZ, 2, 2 * tokens, block), BF16),
            dma((4,)),
            dma((NZ, 2)),
            dma((NZ, 2)),
            dma((NZ, 2)),
            dma((2,)),
            dma((2,)),
            dma((GROUPS,)),
            dma((GROUPS,)),
            dma((GROUPS,)),
            dma((GROUPS,)),
            dma((NZ,)),
            dma((NZ,)),
            dma((NZ, NX)),
            dma((NZ, NX)),
            dma((NZ, 2)),
            dma((NZ, 2)),
            dma((NZ, 2)),
            dma((NZ, 2)),
            dma((2, 7)),
            dma((2, 7)),
            dma((2,)),
            dma((2,)),
            dma((NZ, 2)),
            dma((NZ, 2)),
            dma((NZ, 2)),
        ],
        compiler_params=pltpu.CompilerParams(
            collective_id=0, has_side_effects=True, vmem_limit_bytes=52 * 2**20
        ),
        cost_estimate=pl.CostEstimate(
            flops=6 * tokens * width * kw, bytes_accessed=16 * 2**20, transcendentals=0
        ),
    )(delta_codes[0], master_weights, outer_momentum, activations, key_cotangent)
    return weights, moved, keys, grads, wgrad.T[None]


def solution(mesh):
    placed = (
        P("group", "fsdp", None),
        P("fsdp", None),
        P("fsdp", None),
        P(("group", "fsdp"), None),
        P(("group", "fsdp"), None),
    )
    return jax.shard_map(
        body,
        mesh=mesh,
        in_specs=placed,
        out_specs=(
            P("fsdp", None),
            P("fsdp", None),
            P(("group", "fsdp"), None),
            P(("group", "fsdp"), None),
            P("group", "fsdp", None),
        ),
        check_vma=False,
    )
```

time: 438 us -> 88.9 us (0.20)
  waiting for transfers between devices: 370 us -> 0 us
  Pallas kernels: 0 us -> 78.2 us
  matrix products: 26.1 us -> 0 us
  other arithmetic: 15.4 us -> 0 us
  between operations: 13.8 us -> 0.65 us
    reduce_scatter x1 -> x0, waiting for transfers between devices: 195 us -> none  [body(): lax.psum_scatter(lax.dot_general(features, key_cotangent, (((0,), (0,)),...]
    all_gather x1 -> x0, waiting for transfers between devices: 97 us -> none  [body(): piece = lax.all_gather(inner_weights, 'fsdp', axis=0, tiled=True)]
    pallas_call x0 -> x1, Pallas kernels: none -> 78.2 us  [body(): pl.pallas_call(kernel, name='outer_step', out_shape=(jax.ShapeDtypeStruct...]
    psum x1 -> x0, waiting for transfers between devices: 78 us -> none  [body(): lax.psum(dequantized.astype(jnp.bfloat16), 'group').astype(jnp.float32)]
    dot_general x3 -> x0, matrix products: 26.1 us -> none  [the longest x1 10.3 us: body(): lax.dot_general(features, key_cotangent, (((0,), (0,)), ((), ())), prefer...]
    convert_element_type x2 -> x0, other arithmetic: 9.68 us -> none  [the longest x1 7.17 us: body(): dequantized.astype(jnp.bfloat16)]
    reduce_max x1 -> x0, other arithmetic: 4.39 us -> none  [dequantize(): largest = jnp.max(jnp.abs(blocks), axis=-1, keepdims=True)]
    unnamed x4 -> x7, local copies, waits for them, and re-layouts: 7.19 us -> 9.91 us
  transfers between devices with their start and end apart: 3 -> 0, of which waited for: 3 -> 0; matrix products, arithmetic and copies ran while one was open for 8% -> 0% of each run, Pallas kernels for 0% -> 0%
where the time goes in v1:
time: 88.9 us; the launch traced here: 88.7 us
  Pallas kernels  78.2 us (88%)
  local copies, waits for them, and re-layouts  9.91 us (11%)
    pallas_call x1, Pallas kernels, body(): pl.pallas_call(kernel, name='outer_step', out_shape=(jax.ShapeDtypeStruct...  78.2 us
    unnamed x7, local copies, waits for them, and re-layouts  9.91 us

profile of v1, /device:TPU:1, one launch (start us, length us, event | category | flops | bytes accessed | tf_op | source)
XLA Modules:
  0.0 88.7 jit_solution(14661613849944906378)
XLA Ops:
  0.6 0.0 copy-start
  0.6 0.9 %copy-done = bf16[256,512]{1,0:T(8,128)(2,1)S(1)} copy-done((bf16[256,512]{1,0:T(8,128)(2,1)S(1)}, bf16[256,512]{1,0:T(8,128)(2,1)}, u32[]{:S(2)}) %copy-start) | copy-done | bytes 262168
  1.6 78.2 %outer_step.1 = (f32[256,512]{1,0:T(8,128)S(1)}, f32[256,512]{1,0:T(8,128)S(1)}, bf16[256,512]{1,0:T(8,128)(2,1)S(1)}, bf16[256,8192]{1,0:T(8,128)(2,1)}, f32[512,256]{1,0:T(8,128)}) custom-call(s32[256,512]{1,0:T(8,128)} %bitcast.5, f32[256,512]{1,0:T(8,128)} %master_hbm.1, f32[256,512]{1,0:T(8,128)} %momentum_hbm.1, bf16[256,8192]{1,0:T(8,128)(2,1)} %acts_hbm.1, ...), custom_call_target="tpu_custom_call" | custom-call | flops 6442450944 | bytes 16777216 | tf_op jit(solution)/shard_map/outer_step/pallas_call | solution.py:412
  79.8 2.0 %copy.10 = f32[1,256,512]{2,1,0:T(8,128)} copy(f32[1,256,512]{1,2,0:T(8,128)} %bitcast.4) | data formatting | bytes 1048576
  81.8 0.8 copy.15
  82.6 0.8 copy.16
  83.4 0.7 copy.17
  84.1 4.6 %copy.18 = bf16[256,8192]{1,0:T(8,128)(2,1)} copy(bf16[256,8192]{1,0:T(8,128)(2,1)} %get-tuple-element.28) | data formatting | bytes 8388608
Async XLA Ops:
  0.6 1.0 %copy-start = (bf16[256,512]{1,0:T(8,128)(2,1)S(1)}, bf16[256,512]{1,0:T(8,128)(2,1)}, u32[]{:S(2)}) copy-start(bf16[256,512]{1,0:T(8,128)(2,1)} %cot_hbm.1) | copy-start | bytes 786436

commit v2 on v1

--- a/solution.py
+++ b/solution.py
@@ -12,6 +12,7 @@
 BF16 = jnp.bfloat16
 NX, NY, NZ = 4, 4, 8
 GROUPS = 8
+LAG_Y, LAG_F, LAG_END = 1, 3, 5
 
 
 def device(x, y, z, c):
@@ -41,7 +42,7 @@
 
 def kernel(
     delta_hbm, master_hbm, momentum_hbm, acts_hbm, cot_hbm,
-    weights_out, moved_out, keys_out, grads_hbm, wgrad_out,
+    weights_out, moved_out, keys_out, grads, wgrad_out,
     delta, master, momentum, cot, cot_t, acts,
     coded, coded_in, total, gathered,
     chain_out, chain_in, cross_out, cross_in, cross_own,
@@ -50,7 +51,7 @@
     coded_send, coded_recv, total_send, total_recv,
     z_send, z_recv, x_send, x_recv, y_send, y_recv, f_send, f_recv,
     chain_send, chain_recv, cross_send, cross_recv,
-    back_store, back_send, back_recv,
+    back_send, back_recv,
 ):
     tokens, width = acts_hbm.shape
     kw = cot_hbm.shape[1]
@@ -123,21 +124,15 @@
     barrier = pltpu.get_barrier_semaphore()
     for partner in partners:
         pl.semaphore_signal(barrier, inc=1, device_id=partner, device_id_type=MESH)
-    pl.semaphore_wait(barrier, len(partners))
-
-    cot_swap = remote(cot_hbm, cot.at[tokens_of(c)], pair_send.at[0], pair_recv.at[0], sibling)
-    cot_swap.start()
-
-    @pl.loop(0, NZ)
-    def _(i):
-        for hi in range(2):
-            act_swap(far(i), hi).start()
 
     loads[0].wait()
     for j in range(GROUPS):
         for k in range(kw // 128):
             codes = delta[pl.ds(j * piece, piece), pl.ds(k * 128, 128)]
             coded[j, :, pl.ds(k * 128, 128)] = dequantize(codes).astype(BF16)
+    loads[1].wait()
+    cot_t[c] = cot[tokens_of(c), :].T.reshape(2, half, tokens)
+    pl.semaphore_wait(barrier, len(partners))
 
     def coded_copy(d):
         j = up(g, d, GROUPS)
@@ -150,9 +145,16 @@
     def _(d):
         coded_copy(d).start()
 
-    loads[1].wait()
-    remote(cot_hbm, cot.at[tokens_of(other)], pair_send.at[0], pair_recv.at[0], sibling).wait_recv()
-    cot_t[...] = cot[...].T.reshape(2, half, 2 * tokens)
+    cot_swap = remote(cot_hbm, cot.at[tokens_of(c)], pair_send.at[0], pair_recv.at[0], sibling)
+    cot_swap.start()
+    cot_t_swap = remote(cot_t.at[c], cot_t.at[c], pair_send.at[2], pair_recv.at[2], sibling)
+    cot_t_swap.start()
+
+    @pl.loop(0, NZ)
+    def _(i):
+        for hi in range(2):
+            act_swap(far(i), hi).start()
+
 
     def acts_ready(zz):
         for hi in range(2):
@@ -166,7 +168,8 @@
         )
 
     def share(h, zz, hi):
-        return jnp.dot(cot_t[h], acts[zz, hi], preferred_element_type=F32)
+        turned = jnp.concatenate([cot_t[0, h], cot_t[1, h]], axis=1)
+        return jnp.dot(turned, acts[zz, hi], preferred_element_type=F32)
 
     def chain(k, first):
         s = lax.div(k + 1, 2)
@@ -182,6 +185,7 @@
                 chain_out[way, k, hi] = sent.astype(BF16)
             chain_copy(way, k).start()
 
+    remote(cot_t.at[other], cot_t.at[other], pair_send.at[2], pair_recv.at[2], sibling).wait_recv()
     acts_ready(far(0))
     chain(0, True)
 
@@ -260,6 +264,7 @@
     acts_ready(far(1))
     acts_ready(far(2))
     chain(1, True)
+    remote(cot_hbm, cot.at[tokens_of(other)], pair_send.at[0], pair_recv.at[0], sibling).wait_recv()
 
     @pl.loop(3, NZ)
     def _(i):
@@ -270,31 +275,27 @@
 
     keys[...] = jnp.zeros_like(keys)
 
-    def back_local(zz, hi):
-        return pltpu.make_async_copy(
-            back.at[zz, hi, tokens_of(c)], grads_hbm.at[:, columns(hi, zz, c)], back_store.at[zz, hi]
-        )
-
     def back_copy(zz, hi):
         return remote(
-            back.at[zz, hi, tokens_of(other)], grads_hbm.at[:, columns(hi, zz, c)],
-            back_send.at[zz, hi], back_recv.at[zz, hi], sibling,
+            back.at[zz, hi], grads.at[:, columns(hi, zz, c)], back_send.at[zz, hi], back_recv.at[zz, hi], sibling
         )
 
     def back_arrived(zz, hi):
         return remote(
-            back.at[zz, hi, tokens_of(other)], grads_hbm.at[:, columns(hi, zz, other)],
-            back_send.at[zz, hi], back_recv.at[zz, hi], sibling,
-        )
+            back.at[zz, hi], grads.at[:, columns(hi, zz, other)], back_send.at[zz, hi], back_recv.at[zz, hi], sibling
+        )
+
+    def back_of(rows, w):
+        product = lax.dot_general(rows, w, (((1,), (1,)), ((), ())), preferred_element_type=F32)
+        return (product * out_scale).astype(BF16)
 
     def multiply(zz):
         for hi in range(2):
             lower = [gathered[zz, :, 2 * hi + lo].reshape(block // 2, kw) for lo in range(2)]
             w = jnp.concatenate(lower, axis=0)
-            grads = lax.dot_general(cot[...], w, (((1,), (1,)), ((), ())), preferred_element_type=F32)
-            back[zz, hi] = (grads * out_scale).astype(BF16)
+            back[zz, hi] = back_of(cot[tokens_of(other), :], w)
             back_copy(zz, hi).start()
-            back_local(zz, hi).start()
+            grads[:, columns(hi, zz, c)] = back_of(cot[tokens_of(c), :], w)
             keys[...] += jnp.dot(acts[zz, hi], w, preferred_element_type=F32)
 
     def cross_copy(h):
@@ -316,7 +317,17 @@
                     cross_out[h] = done.astype(BF16)
                     cross_copy(h).start()
 
-    @pl.loop(1, NZ + 3)
+    def outer_results():
+        for j in range(GROUPS):
+            @pl.when(g != j)
+            def _():
+                total_arrived(j).wait_recv()
+
+        for j in range(GROUPS):
+            own = pl.ds(j * piece, piece)
+            weights_out[own, :], moved_out[own, :] = nesterov(total[j], master[own, :], momentum[own, :])
+
+    @pl.loop(1, NZ + LAG_END)
     def _(i):
         @pl.when(i < NZ)
         def _():
@@ -325,17 +336,17 @@
             for d in range(1, NX):
                 x_copy(zz, d).start()
 
-        @pl.when(i < NZ + 1)
-        def _():
-            zz = wave(i - 1)
+        @pl.when(i < NZ + LAG_Y)
+        def _():
+            zz = wave(i - LAG_Y)
             for d in range(1, NX):
                 x_arrived(zz, up(x, d, NX)).wait_recv()
             for way in range(2):
                 y_copy(zz, way).start()
 
-        @pl.when(jnp.logical_and(i >= 2, i < NZ + 2))
-        def _():
-            zz = wave(i - 2)
+        @pl.when(jnp.logical_and(i >= LAG_F, i < NZ + LAG_F))
+        def _():
+            zz = wave(i - LAG_F)
             for way in range(2):
                 y_arrived(zz, way).wait_recv()
             for way in range(2):
@@ -349,9 +360,13 @@
         def _():
             chain_end()
 
-        @pl.when(i >= 3)
-        def _():
-            zz = wave(i - 3)
+        @pl.when(i == 3)
+        def _():
+            outer_results()
+
+        @pl.when(i >= LAG_END)
+        def _():
+            zz = wave(i - LAG_END)
             for way in range(2):
                 f_arrived(zz, way).wait_recv()
             multiply(zz)
@@ -359,15 +374,6 @@
     keys_copy = remote(keys.at[tokens_of(other)], keys_in, pair_send.at[1], pair_recv.at[1], sibling)
     keys_copy.start()
 
-    for j in range(GROUPS):
-        @pl.when(g != j)
-        def _():
-            total_arrived(j).wait_recv()
-
-    for j in range(GROUPS):
-        own = pl.ds(j * piece, piece)
-        weights_out[own, :], moved_out[own, :] = nesterov(total[j], master[own, :], momentum[own, :])
-
     for h in range(2):
         cross_copy(h).wait_recv()
         wgrad_out[pl.ds(h * half, half), :] = (cross_own[h] + cross_in[h].astype(F32)) * out_scale
@@ -376,6 +382,7 @@
     keys_out[...] = ((keys[tokens_of(c), :] + keys_in[...]) * out_scale).astype(BF16)
 
     cot_swap.wait_send()
+    cot_t_swap.wait_send()
     keys_copy.wait_send()
     for h in range(2):
         cross_copy(h).wait_send()
@@ -384,7 +391,6 @@
     def _(zz):
         for hi in range(2):
             act_swap(zz, hi).wait_send()
-            back_local(zz, hi).wait()
             back_copy(zz, hi).wait_send()
             back_arrived(zz, hi).wait_recv()
         for d in range(1, NX):
@@ -402,6 +408,17 @@
             chain_copy(way, d - 1).wait_send()
 
 
+def finish(weights, moved, keys, grads, turned, weights_hbm, moved_hbm, keys_hbm, grads_hbm, wgrad_hbm, wgrad, sem):
+    pairs = ((grads, grads_hbm), (weights, weights_hbm), (moved, moved_hbm), (keys, keys_hbm), (wgrad, wgrad_hbm))
+    copies = [pltpu.make_async_copy(src, dst, sem.at[i]) for i, (src, dst) in enumerate(pairs)]
+    for copy in copies[:4]:
+        copy.start()
+    wgrad[...] = turned[...].T
+    copies[4].start()
+    for copy in copies:
+        copy.wait()
+
+
 def body(delta_codes, master_weights, outer_momentum, activations, key_cotangent):
     tokens, width = activations.shape
     rows, kw = master_weights.shape
@@ -409,24 +426,25 @@
     dma = pltpu.SemaphoreType.DMA
     hbm = pl.BlockSpec(memory_space=pl.ANY)
     vmem = pl.BlockSpec(memory_space=pltpu.VMEM)
-    weights, moved, keys, grads, wgrad = pl.pallas_call(
+    arguments = (delta_codes[0], master_weights, outer_momentum, activations, key_cotangent)
+    results = pl.pallas_call(
         kernel,
         name="outer_step",
         out_shape=(
-            jax.ShapeDtypeStruct((rows, kw), F32),
-            jax.ShapeDtypeStruct((rows, kw), F32),
-            jax.ShapeDtypeStruct((tokens, kw), BF16),
-            jax.ShapeDtypeStruct((tokens, width), BF16),
-            jax.ShapeDtypeStruct((kw, block), F32),
+            pltpu.VMEM((rows, kw), F32),
+            pltpu.VMEM((rows, kw), F32),
+            pltpu.VMEM((tokens, kw), BF16),
+            pltpu.VMEM((tokens, width), BF16),
+            pltpu.VMEM((kw, block), F32),
         ),
         in_specs=[hbm] * 5,
-        out_specs=(vmem, vmem, vmem, hbm, vmem),
+        out_specs=(vmem,) * 5,
         scratch_shapes=[
             pltpu.VMEM((rows, kw), jnp.int32),
             pltpu.VMEM((rows, kw), F32),
             pltpu.VMEM((rows, kw), F32),
             pltpu.VMEM((2 * tokens, kw), BF16),
-            pltpu.VMEM((2, half, 2 * tokens), BF16),
+            pltpu.VMEM((2, 2, half, tokens), BF16),
             pltpu.VMEM((NZ, 2, 2 * tokens, block), BF16),
             pltpu.VMEM((GROUPS, piece, kw), BF16),
             pltpu.VMEM((GROUPS, piece, kw), BF16),
@@ -439,13 +457,13 @@
             pltpu.VMEM((2, half, block), F32),
             pltpu.VMEM((2 * tokens, kw), F32),
             pltpu.VMEM((tokens, kw), F32),
-            pltpu.VMEM((NZ, 2, 2 * tokens, block), BF16),
+            pltpu.VMEM((NZ, 2, tokens, block), BF16),
             dma((4,)),
             dma((NZ, 2)),
             dma((NZ, 2)),
             dma((NZ, 2)),
-            dma((2,)),
-            dma((2,)),
+            dma((3,)),
+            dma((3,)),
             dma((GROUPS,)),
             dma((GROUPS,)),
             dma((GROUPS,)),
@@ -464,16 +482,30 @@
             dma((2,)),
             dma((NZ, 2)),
             dma((NZ, 2)),
-            dma((NZ, 2)),
         ],
         compiler_params=pltpu.CompilerParams(
-            collective_id=0, has_side_effects=True, vmem_limit_bytes=52 * 2**20
+            collective_id=0, has_side_effects=True, vmem_limit_bytes=44 * 2**20
         ),
         cost_estimate=pl.CostEstimate(
             flops=6 * tokens * width * kw, bytes_accessed=16 * 2**20, transcendentals=0
         ),
-    )(delta_codes[0], master_weights, outer_momentum, activations, key_cotangent)
-    return weights, moved, keys, grads, wgrad.T[None]
+    )(*[pltpu.with_memory_space_constraint(a, pltpu.HBM) for a in arguments])
+    weights, moved, keys, grads, wgrad = pl.pallas_call(
+        finish,
+        name="finish",
+        out_shape=(
+            jax.ShapeDtypeStruct((rows, kw), F32),
+            jax.ShapeDtypeStruct((rows, kw), F32),
+            jax.ShapeDtypeStruct((tokens, kw), BF16),
+            jax.ShapeDtypeStruct((tokens, width), BF16),
+            jax.ShapeDtypeStruct((rows, kw), F32),
+        ),
+        in_specs=[vmem] * 5,
+        out_specs=(hbm,) * 5,
+        scratch_shapes=[pltpu.VMEM((rows, kw), F32), dma((5,))],
+        compiler_params=pltpu.CompilerParams(vmem_limit_bytes=16 * 2**20),
+    )(*[pltpu.with_memory_space_constraint(r, pltpu.VMEM) for r in results])
+    return weights, moved, keys, grads, wgrad[None]
 
 
 def solution(mesh):

time: 88.9 us -> 81.2 us (0.913)
  local copies, waits for them, and re-layouts: 9.91 us -> 0 us
  Pallas kernels: 78.2 us -> 80.5 us
    unnamed x7 -> x0, local copies, waits for them, and re-layouts: 9.91 us -> none
    pallas_call x1 -> x2, Pallas kernels: 78.2 us -> 80.5 us  [the longest x1 77.9 us: body(): pl.pallas_call(kernel, name='outer_step', out_shape=(pltpu.VMEM((rows, kw...]
where the time goes in v2:
time: 81.2 us
  Pallas kernels  80.5 us (99%)
    pallas_call x1, Pallas kernels, body(): pl.pallas_call(kernel, name='outer_step', out_shape=(pltpu.VMEM((rows, kw...  77.9 us
    pallas_call x1, Pallas kernels, body(): pl.pallas_call(finish, name='finish', out_shape=(jax.ShapeDtypeStruct((ro...  2.61 us

profile of v2, /device:TPU:1, one launch (start us, length us, event | category | flops | bytes accessed | tf_op | source)
XLA Modules:
  0.0 81.2 jit_solution(9047601952466659401)
XLA Ops:
  0.6 77.9 %outer_step.1 = (f32[256,512]{1,0:T(8,128)S(1)}, f32[256,512]{1,0:T(8,128)S(1)}, bf16[256,512]{1,0:T(8,128)(2,1)S(1)}, bf16[256,8192]{1,0:T(8,128)(2,1)S(1)}, f32[512,256]{1,0:T(8,128)S(1)}) custom-call(s32[256,512]{1,0:T(8,128)} %bitcast.2, f32[256,512]{1,0:T(8,128)} %master_hbm.1, f32[256,512]{1,0:T(8,128)} %momentum_hbm.1, bf16[256,8192]{1,0:T(8,128)(2,1)} %acts_hbm.1, ...), custom_call_target="tpu_custom_call" | custom-call | flops 6442450944 | bytes 16777216 | tf_op jit(solution)/shard_map/outer_step/pallas_call | solution.py:430
  78.5 2.6 %finish.1 = (f32[256,512]{1,0:T(8,128)}, f32[256,512]{1,0:T(8,128)}, bf16[256,512]{1,0:T(8,128)(2,1)}, bf16[256,8192]{1,0:T(8,128)(2,1)}, f32[256,512]{1,0:T(8,128)}) custom-call(f32[256,512]{1,0:T(8,128)S(1)} %get-tuple-element.15.weights, f32[256,512]{1,0:T(8,128)S(1)} %get-tuple-element.16.moved, bf16[256,512]{1,0:T(8,128)(2,1)S(1)} %get-tuple-element.17.keys, ...), custom_call_target="tpu_custom_call" | custom-call | tf_op jit(solution)/shard_map/finish/pallas_call | solution.py:493

commit v3 on v2

--- a/solution.py
+++ b/solution.py
@@ -13,6 +13,7 @@
 NX, NY, NZ = 4, 4, 8
 GROUPS = 8
 LAG_Y, LAG_F, LAG_END = 1, 3, 5
+CROSS_FIRST = 96
 
 
 def device(x, y, z, c):
@@ -43,14 +44,16 @@
 def kernel(
     delta_hbm, master_hbm, momentum_hbm, acts_hbm, cot_hbm,
     weights_out, moved_out, keys_out, grads, wgrad_out,
-    delta, master, momentum, cot, cot_t, acts,
+    delta, master, momentum, cot, cot_t, late_t, early_t, acts,
     coded, coded_in, total, gathered,
     chain_out, chain_in, cross_out, cross_in, cross_own,
+    first_out, first_in, line_out, line_in,
     keys, keys_in, back,
     load_sem, acts_load, acts_send, acts_recv, pair_send, pair_recv,
     coded_send, coded_recv, total_send, total_recv,
     z_send, z_recv, x_send, x_recv, y_send, y_recv, f_send, f_recv,
     chain_send, chain_recv, cross_send, cross_recv,
+    first_send, first_recv, line_send, line_recv,
     back_send, back_recv,
 ):
     tokens, width = acts_hbm.shape
@@ -58,6 +61,7 @@
     block = width // 32
     piece = block // GROUPS
     half = kw // 2
+    late = half - CROSS_FIRST
     out_scale = width ** (-0.5)
 
     g, f = lax.axis_index("group"), lax.axis_index("fsdp")
@@ -117,7 +121,7 @@
             act_load(far(i), hi).start()
 
     partners = [sibling]
-    partners += [device(x, y, up(z, d, NZ), c) for d in range(1, NZ)]
+    partners += [device(x, y, up(z, d, NZ), c) for d in (1, NZ - 1)]
     partners += [device(up(x, d, NX), y, z, c) for d in range(1, NX)]
     partners += [device(x, up(y, d, NY), z, c) for d in range(1, NY)]
     partners += [device(2 * x_hi + 1 - x_lo, up(y, d, NY), z, c) for d in range(1, NY)]
@@ -168,8 +172,48 @@
         )
 
     def share(h, zz, hi):
-        turned = jnp.concatenate([cot_t[0, h], cot_t[1, h]], axis=1)
-        return jnp.dot(turned, acts[zz, hi], preferred_element_type=F32)
+        return jnp.dot(late_t[h], acts[zz, hi], preferred_element_type=F32)
+
+    def early_share(h, zz, hi):
+        return jnp.dot(early_t[h], acts[zz, hi], preferred_element_type=F32)
+
+    def first_copy(zz):
+        return remote(
+            first_out.at[zz], first_in.at[zz], first_send.at[zz], first_recv.at[zz], device(up(x, 2, NX), y, z, c)
+        )
+
+    def first(i):
+        zz = far(i)
+        for h in range(2):
+            first_out[zz, h] = early_share(h, zz, 1 - x_hi).astype(BF16)
+        first_copy(zz).start()
+
+    def line_copy(way, k):
+        to = device(x, y, up(z, 1 if way == 0 else NZ - 1, NZ), c)
+        return remote(line_out.at[way, k], line_in.at[way, k], line_send.at[way, k], line_recv.at[way, k], to)
+
+    def line(k, opening):
+        s = lax.div(k + 1, 2)
+        for way in range(2):
+            zz = up(z, 4 - s if way == 0 else 4 + s, NZ)
+            h = lax.rem(k + way, 2)
+            if not opening:
+                line_copy(way, k - 2).wait_recv()
+            sent = early_share(h, zz, x_hi) + first_in[zz, h].astype(F32)
+            if not opening:
+                sent += line_in[way, k - 2].astype(F32)
+            line_out[way, k] = sent.astype(BF16)
+            line_copy(way, k).start()
+
+    def line_end():
+        first_copy(z).wait_recv()
+        for way in range(2):
+            for k in (5, 6):
+                line_copy(way, k).wait_recv()
+        for h in range(2):
+            done = early_share(h, z, x_hi) + first_in[z, h].astype(F32)
+            done += line_in[0, 6 - h].astype(F32) + line_in[1, 5 + h].astype(F32)
+            wgrad_out[pl.ds(h * half + late, CROSS_FIRST), :] = done * out_scale
 
     def chain(k, first):
         s = lax.div(k + 1, 2)
@@ -186,8 +230,13 @@
             chain_copy(way, k).start()
 
     remote(cot_t.at[other], cot_t.at[other], pair_send.at[2], pair_recv.at[2], sibling).wait_recv()
+    for h in range(2):
+        for core in range(2):
+            late_t[h, :, pl.ds(core * tokens, tokens)] = cot_t[core, h, :late]
+            early_t[h, :, pl.ds(core * tokens, tokens)] = cot_t[core, h, late:]
     acts_ready(far(0))
     chain(0, True)
+    first(0)
 
     rows = pl.ds(pl.multiple_of(g * piece, piece), piece)
 
@@ -204,14 +253,12 @@
     updated, _ = nesterov(total[g], master[rows, :], momentum[rows, :])
     gathered[z, y, x] = updated.astype(BF16)
 
-    def z_copy(d):
-        return remote(
-            gathered.at[z, y, x], gathered.at[z, y, x], z_send.at[d], z_recv.at[z],
-            device(x, y, up(z, d, NZ), c),
-        )
+    def z_copy(zz, way):
+        to = device(x, y, up(z, 1 if way == 0 else NZ - 1, NZ), c)
+        return remote(gathered.at[zz, y, x], gathered.at[zz, y, x], z_send.at[zz, way], z_recv.at[zz], to)
 
     def z_arrived(zz):
-        return remote(gathered.at[zz, y, x], gathered.at[zz, y, x], z_send.at[0], z_recv.at[zz], sibling)
+        return remote(gathered.at[zz, y, x], gathered.at[zz, y, x], z_send.at[zz, 0], z_recv.at[zz], sibling)
 
     def x_copy(zz, d):
         return remote(
@@ -244,8 +291,8 @@
         part = gathered.at[zz, up(y, 2, NY), pl.ds(way * 2, 2)]
         return remote(part, part, f_send.at[zz, way], f_recv.at[zz, way], sibling)
 
-    for d in (1, 7, 2, 6, 3, 5, 4):
-        z_copy(d).start()
+    for way in range(2):
+        z_copy(z, way).start()
     for d in range(1, NX):
         x_copy(z, d).start()
 
@@ -264,6 +311,8 @@
     acts_ready(far(1))
     acts_ready(far(2))
     chain(1, True)
+    first(1)
+    first(2)
     remote(cot_hbm, cot.at[tokens_of(other)], pair_send.at[0], pair_recv.at[0], sibling).wait_recv()
 
     @pl.loop(3, NZ)
@@ -333,6 +382,15 @@
         def _():
             zz = wave(i)
             z_arrived(zz).wait_recv()
+
+            @pl.when(jnp.logical_and(lax.rem(i, 2) == 1, i < 7))
+            def _():
+                z_copy(zz, 1).start()
+
+            @pl.when(jnp.logical_and(lax.rem(i, 2) == 0, i < 6))
+            def _():
+                z_copy(zz, 0).start()
+
             for d in range(1, NX):
                 x_copy(zz, d).start()
 
@@ -355,10 +413,35 @@
         @pl.when(i < 6)
         def _():
             chain(i + 1, False)
+            first(i + 2)
+
+        @pl.when(i == 1)
+        def _():
+            first_copy(far(0)).wait_recv()
+            line(0, True)
+
+        @pl.when(i == 2)
+        def _():
+            first_copy(far(1)).wait_recv()
+            first_copy(far(2)).wait_recv()
+            line(1, True)
+
+        @pl.when(jnp.logical_or(i == 4, i == 6))
+        def _():
+            first_copy(far(i - 1)).wait_recv()
+            first_copy(far(i)).wait_recv()
+
+        @pl.when(jnp.logical_and(i >= 3, i < 8))
+        def _():
+            line(i - 1, False)
 
         @pl.when(i == 7)
         def _():
             chain_end()
+
+        @pl.when(i == 9)
+        def _():
+            line_end()
 
         @pl.when(i == 3)
         def _():
@@ -376,7 +459,7 @@
 
     for h in range(2):
         cross_copy(h).wait_recv()
-        wgrad_out[pl.ds(h * half, half), :] = (cross_own[h] + cross_in[h].astype(F32)) * out_scale
+        wgrad_out[pl.ds(h * half, late), :] = (cross_own[h] + cross_in[h].astype(F32)) * out_scale
 
     keys_copy.wait_recv()
     keys_out[...] = ((keys[tokens_of(c), :] + keys_in[...]) * out_scale).astype(BF16)
@@ -393,19 +476,28 @@
             act_swap(zz, hi).wait_send()
             back_copy(zz, hi).wait_send()
             back_arrived(zz, hi).wait_recv()
+        first_copy(zz).wait_send()
         for d in range(1, NX):
             x_copy(zz, d).wait_send()
         for way in range(2):
             y_copy(zz, way).wait_send()
             f_copy(zz, way).wait_send()
 
+    @pl.loop(0, 4)
+    def _(d):
+        z_copy(up(z, d, NZ), 1).wait_send()
+
+    @pl.loop(0, 3)
+    def _(d):
+        z_copy(up(z, NZ - d, NZ), 0).wait_send()
+
     @pl.loop(1, NZ)
     def _(d):
         coded_copy(d).wait_send()
         total_copy(d).wait_send()
-        z_copy(d).wait_send()
         for way in range(2):
             chain_copy(way, d - 1).wait_send()
+            line_copy(way, d - 1).wait_send()
 
 
 def finish(weights, moved, keys, grads, turned, weights_hbm, moved_hbm, keys_hbm, grads_hbm, wgrad_hbm, wgrad, sem):
@@ -423,6 +515,7 @@
     tokens, width = activations.shape
     rows, kw = master_weights.shape
     block, piece, half = width // 32, width // 32 // GROUPS, kw // 2
+    late = half - CROSS_FIRST
     dma = pltpu.SemaphoreType.DMA
     hbm = pl.BlockSpec(memory_space=pl.ANY)
     vmem = pl.BlockSpec(memory_space=pltpu.VMEM)
@@ -445,16 +538,22 @@
             pltpu.VMEM((rows, kw), F32),
             pltpu.VMEM((2 * tokens, kw), BF16),
             pltpu.VMEM((2, 2, half, tokens), BF16),
+            pltpu.VMEM((2, late, 2 * tokens), BF16),
+            pltpu.VMEM((2, CROSS_FIRST, 2 * tokens), BF16),
             pltpu.VMEM((NZ, 2, 2 * tokens, block), BF16),
             pltpu.VMEM((GROUPS, piece, kw), BF16),
             pltpu.VMEM((GROUPS, piece, kw), BF16),
             pltpu.VMEM((GROUPS, piece, kw), BF16),
             pltpu.VMEM((NZ, NY, NX, piece, kw), BF16),
-            pltpu.VMEM((2, 7, 2, half, block), BF16),
-            pltpu.VMEM((2, 7, 2, half, block), BF16),
-            pltpu.VMEM((2, half, block), BF16),
-            pltpu.VMEM((2, half, block), BF16),
-            pltpu.VMEM((2, half, block), F32),
+            pltpu.VMEM((2, 7, 2, late, block), BF16),
+            pltpu.VMEM((2, 7, 2, late, block), BF16),
+            pltpu.VMEM((2, late, block), BF16),
+            pltpu.VMEM((2, late, block), BF16),
+            pltpu.VMEM((2, late, block), F32),
+            pltpu.VMEM((NZ, 2, CROSS_FIRST, block), BF16),
+            pltpu.VMEM((NZ, 2, CROSS_FIRST, block), BF16),
+            pltpu.VMEM((2, 7, CROSS_FIRST, block), BF16),
+            pltpu.VMEM((2, 7, CROSS_FIRST, block), BF16),
             pltpu.VMEM((2 * tokens, kw), F32),
             pltpu.VMEM((tokens, kw), F32),
             pltpu.VMEM((NZ, 2, tokens, block), BF16),
@@ -468,7 +567,7 @@
             dma((GROUPS,)),
             dma((GROUPS,)),
             dma((GROUPS,)),
-            dma((NZ,)),
+            dma((NZ, 2)),
             dma((NZ,)),
             dma((NZ, NX)),
             dma((NZ, NX)),
@@ -480,6 +579,10 @@
             dma((2, 7)),
             dma((2,)),
             dma((2,)),
+            dma((NZ,)),
+            dma((NZ,)),
+            dma((2, 7)),
+            dma((2, 7)),
             dma((NZ, 2)),
             dma((NZ, 2)),
         ],

time: 81.2 us -> 72.8 us (0.90)
  Pallas kernels: 80.5 us -> 72.1 us
    pallas_call x1, Pallas kernels: 77.9 us -> 69.5 us  [body(): pl.pallas_call(kernel, name='outer_step', out_shape=(pltpu.VMEM((rows, kw...]
where the time goes in v3:
time: 72.8 us
  Pallas kernels  72.1 us (99%)
    pallas_call x1, Pallas kernels, body(): pl.pallas_call(kernel, name='outer_step', out_shape=(pltpu.VMEM((rows, kw...  69.5 us
    pallas_call x1, Pallas kernels, body(): pl.pallas_call(finish, name='finish', out_shape=(jax.ShapeDtypeStruct((ro...  2.61 us

profile of v3, /device:TPU:1, one launch (start us, length us, event | category | flops | bytes accessed | tf_op | source)
XLA Modules:
  0.0 72.8 jit_solution(12282969174425518080)
XLA Ops:
  0.6 69.5 %outer_step.1 = (f32[256,512]{1,0:T(8,128)S(1)}, f32[256,512]{1,0:T(8,128)S(1)}, bf16[256,512]{1,0:T(8,128)(2,1)S(1)}, bf16[256,8192]{1,0:T(8,128)(2,1)S(1)}, f32[512,256]{1,0:T(8,128)S(1)}) custom-call(s32[256,512]{1,0:T(8,128)} %bitcast.2, f32[256,512]{1,0:T(8,128)} %master_hbm.1, f32[256,512]{1,0:T(8,128)} %momentum_hbm.1, bf16[256,8192]{1,0:T(8,128)(2,1)} %acts_hbm.1, ...), custom_call_target="tpu_custom_call" | custom-call | flops 6442450944 | bytes 16777216 | tf_op jit(solution)/shard_map/outer_step/pallas_call | solution.py:523
  70.1 2.6 %finish.1 = (f32[256,512]{1,0:T(8,128)}, f32[256,512]{1,0:T(8,128)}, bf16[256,512]{1,0:T(8,128)(2,1)}, bf16[256,8192]{1,0:T(8,128)(2,1)}, f32[256,512]{1,0:T(8,128)}) custom-call(f32[256,512]{1,0:T(8,128)S(1)} %get-tuple-element.15.weights, f32[256,512]{1,0:T(8,128)S(1)} %get-tuple-element.16.moved, bf16[256,512]{1,0:T(8,128)(2,1)S(1)} %get-tuple-element.17.keys, ...), custom_call_target="tpu_custom_call" | custom-call | tf_op jit(solution)/shard_map/finish/pallas_call | solution.py:596

commit v4 on v3

--- a/solution.py
+++ b/solution.py
@@ -13,7 +13,11 @@
 NX, NY, NZ = 4, 4, 8
 GROUPS = 8
 LAG_Y, LAG_F, LAG_END = 1, 3, 5
-CROSS_FIRST = 96
+LINE_EARLY = 0
+TOTAL_AT = 2
+ORDER = ("near", "line", "total", "row", "far", "first", "last", "chain")
+CROSS_FIRST = 80
+TURNED = (4, 6)
 
 
 def device(x, y, z, c):
@@ -165,10 +169,11 @@
             act_load(zz, hi).wait()
             act_arrived(zz, hi).wait_recv()
 
-    def chain_copy(way, k):
+    def chain_copy(way, k, part):
         to = device(x, y, up(z, 1 if way == 0 else NZ - 1, NZ), c)
         return remote(
-            chain_out.at[way, k], chain_in.at[way, k], chain_send.at[way, k], chain_recv.at[way, k], to
+            chain_out.at[way, k, part], chain_in.at[way, k, part],
+            chain_send.at[way, k, part], chain_recv.at[way, k, part], to,
         )
 
     def share(h, zz, hi):
@@ -215,19 +220,18 @@
             done += line_in[0, 6 - h].astype(F32) + line_in[1, 5 + h].astype(F32)
             wgrad_out[pl.ds(h * half + late, CROSS_FIRST), :] = done * out_scale
 
-    def chain(k, first):
+    def chain(k, opening):
         s = lax.div(k + 1, 2)
-        for way in range(2):
-            zz = up(z, 4 - s if way == 0 else 4 + s, NZ)
-            h = lax.rem(k + way, 2)
-            if not first:
-                chain_copy(way, k - 2).wait_recv()
-            for hi in range(2):
-                sent = share(h, zz, hi)
-                if not first:
-                    sent += chain_in[way, k - 2, hi].astype(F32)
-                chain_out[way, k, hi] = sent.astype(BF16)
-            chain_copy(way, k).start()
+        for part in range(2):
+            for way in range(2):
+                zz = up(z, 4 - s if way == 0 else 4 + s, NZ)
+                h = lax.rem(k + way, 2)
+                sent = share(h, zz, x_hi if part else 1 - x_hi)
+                if not opening:
+                    chain_copy(way, k - 2, part).wait_recv()
+                    sent += chain_in[way, k - 2, part].astype(F32)
+                chain_out[way, k, part] = sent.astype(BF16)
+                chain_copy(way, k, part).start()
 
     remote(cot_t.at[other], cot_t.at[other], pair_send.at[2], pair_recv.at[2], sibling).wait_recv()
     for h in range(2):
@@ -260,41 +264,99 @@
     def z_arrived(zz):
         return remote(gathered.at[zz, y, x], gathered.at[zz, y, x], z_send.at[zz, 0], z_recv.at[zz], sibling)
 
-    def x_copy(zz, d):
-        return remote(
-            gathered.at[zz, y, x], gathered.at[zz, y, x], x_send.at[zz, d], x_recv.at[zz, x],
-            device(up(x, d, NX), y, z, c),
-        )
-
-    def x_arrived(zz, xx):
-        return remote(
-            gathered.at[zz, y, xx], gathered.at[zz, y, xx], x_send.at[zz, 0], x_recv.at[zz, xx], sibling
-        )
-
-    def y_copy(zz, way):
-        to = device(x, up(y, 1 if way == 0 else NY - 1, NY), z, c)
-        return remote(gathered.at[zz, y], gathered.at[zz, y], y_send.at[zz, way], y_recv.at[zz, way], to)
-
-    def y_arrived(zz, way):
-        yy = up(y, NY - 1 if way == 0 else 1, NY)
-        return remote(
-            gathered.at[zz, yy], gathered.at[zz, yy], y_send.at[zz, way], y_recv.at[zz, way], sibling
-        )
-
-    def f_copy(zz, way):
-        yy = up(y, NY - 1 if way == 0 else 1, NY)
-        to = device(x, up(y, 1 if way == 0 else NY - 1, NY), z, c)
-        part = gathered.at[zz, yy, pl.ds(way * 2, 2)]
-        return remote(part, part, f_send.at[zz, way], f_recv.at[zz, way], to)
-
-    def f_arrived(zz, way):
-        part = gathered.at[zz, up(y, 2, NY), pl.ds(way * 2, 2)]
+    def near_copy(zz, d, turned):
+        to = device(x, up(y, d, NY), z, c) if turned else device(up(x, d, NX), y, z, c)
+        part = gathered.at[zz, y, x]
+        return remote(part, part, x_send.at[zz, d], x_recv.at[zz, y if turned else x], to)
+
+    def near_arrived(zz, d, turned):
+        at = up(y if turned else x, d, NX)
+        part = gathered.at[zz, at, x] if turned else gathered.at[zz, y, at]
+        return remote(part, part, x_send.at[zz, 0], x_recv.at[zz, at], sibling)
+
+    def neighbour(way, turned):
+        d = 1 if way == 0 else NX - 1
+        return device(up(x, d, NX), y, z, c) if turned else device(x, up(y, d, NY), z, c)
+
+    def line_of(zz, d, turned):
+        return gathered.at[zz, :, up(x, d, NX)] if turned else gathered.at[zz, up(y, d, NY)]
+
+    def half_of(zz, d, way, turned):
+        if turned:
+            return gathered.at[zz, pl.ds(way * 2, 2), up(x, d, NX)]
+        return gathered.at[zz, up(y, d, NY), pl.ds(way * 2, 2)]
+
+    def y_copy(zz, way, turned):
+        part = line_of(zz, 0, turned)
+        return remote(part, part, y_send.at[zz, way], y_recv.at[zz, way], neighbour(way, turned))
+
+    def y_arrived(zz, way, turned):
+        part = line_of(zz, 3 if way == 0 else 1, turned)
+        return remote(part, part, y_send.at[zz, way], y_recv.at[zz, way], sibling)
+
+    def f_copy(zz, way, turned):
+        part = half_of(zz, 3 if way == 0 else 1, way, turned)
+        return remote(part, part, f_send.at[zz, way], f_recv.at[zz, way], neighbour(way, turned))
+
+    def f_arrived(zz, way, turned):
+        part = half_of(zz, 2, way, turned)
         return remote(part, part, f_send.at[zz, way], f_recv.at[zz, way], sibling)
+
+    def either(i, step):
+        if isinstance(i, int):
+            step(i in TURNED)
+            return
+        hit = i == -1
+        for t in TURNED:
+            hit = jnp.logical_or(hit, i == t)
+        pl.when(hit)(lambda: step(True))
+        pl.when(jnp.logical_not(hit))(lambda: step(False))
+
+    def stage_near(i, zz):
+        def step(turned):
+            for d in range(1, NX):
+                near_copy(zz, d, turned).start()
+
+        either(i, step)
+
+    def stage_line(i, zz):
+        def step(turned):
+            for d in range(1, NX):
+                near_arrived(zz, d, turned).wait_recv()
+            for way in range(2):
+                y_copy(zz, way, turned).start()
+
+        either(i, step)
+
+    def stage_far(i, zz):
+        def step(turned):
+            for way in range(2):
+                y_arrived(zz, way, turned).wait_recv()
+            for way in range(2):
+                f_copy(zz, way, turned).start()
+
+        either(i, step)
+
+    def stage_last(i, zz):
+        def step(turned):
+            for way in range(2):
+                f_arrived(zz, way, turned).wait_recv()
+
+        either(i, step)
+
+    def stage_sent(i, zz):
+        def step(turned):
+            for d in range(1, NX):
+                near_copy(zz, d, turned).wait_send()
+            for way in range(2):
+                y_copy(zz, way, turned).wait_send()
+                f_copy(zz, way, turned).wait_send()
+
+        either(i, step)
 
     for way in range(2):
         z_copy(z, way).start()
-    for d in range(1, NX):
-        x_copy(z, d).start()
+    stage_near(0, z)
 
     def total_copy(d):
         return remote(
@@ -303,10 +365,6 @@
 
     def total_arrived(j):
         return remote(total.at[j], total.at[j], total_send.at[0], total_recv.at[j], sibling)
-
-    @pl.loop(1, GROUPS)
-    def _(d):
-        total_copy(d).start()
 
     acts_ready(far(1))
     acts_ready(far(2))
@@ -352,19 +410,18 @@
             cross_out.at[h], cross_in.at[h], cross_send.at[h], cross_recv.at[h], device(up(x, 2, NX), y, z, c)
         )
 
-    def chain_end():
+    def chain_end(part):
         for way in range(2):
             for k in (5, 6):
-                chain_copy(way, k).wait_recv()
-        for mine in range(2):
-            hi = x_hi if mine else 1 - x_hi
-            for h in range(2):
-                done = share(h, z, hi) + chain_in[0, 6 - h, hi].astype(F32) + chain_in[1, 5 + h, hi].astype(F32)
-                if mine:
-                    cross_own[h] = done
-                else:
-                    cross_out[h] = done.astype(BF16)
-                    cross_copy(h).start()
+                chain_copy(way, k, part).wait_recv()
+        for h in range(2):
+            done = share(h, z, x_hi if part else 1 - x_hi)
+            done += chain_in[0, 6 - h, part].astype(F32) + chain_in[1, 5 + h, part].astype(F32)
+            if part:
+                cross_own[h] = done
+            else:
+                cross_out[h] = done.astype(BF16)
+                cross_copy(h).start()
 
     def outer_results():
         for j in range(GROUPS):
@@ -376,45 +433,56 @@
             own = pl.ds(j * piece, piece)
             weights_out[own, :], moved_out[own, :] = nesterov(total[j], master[own, :], momentum[own, :])
 
-    @pl.loop(1, NZ + LAG_END)
-    def _(i):
-        @pl.when(i < NZ)
-        def _():
-            zz = wave(i)
-            z_arrived(zz).wait_recv()
-
-            @pl.when(jnp.logical_and(lax.rem(i, 2) == 1, i < 7))
+    def steps_near(i):
+        for j in (2 * i - 1, 2 * i):
+            @pl.when(j < NZ)
             def _():
-                z_copy(zz, 1).start()
-
-            @pl.when(jnp.logical_and(lax.rem(i, 2) == 0, i < 6))
+                zz = wave(j)
+                z_arrived(zz).wait_recv()
+
+                @pl.when(jnp.logical_and(lax.rem(j, 2) == 1, j < 7))
+                def _():
+                    z_copy(zz, 1).start()
+
+                @pl.when(jnp.logical_and(lax.rem(j, 2) == 0, j < 6))
+                def _():
+                    z_copy(zz, 0).start()
+
+                stage_near(j, zz)
+
+    def steps_line(i):
+        @pl.when(jnp.logical_and(i >= LAG_Y + LINE_EARLY, i < NZ + LAG_Y))
+        def _():
+            stage_line(i - LAG_Y, wave(i - LAG_Y))
+
+    def steps_far(i):
+        @pl.when(jnp.logical_and(i >= LAG_F, i < NZ + LAG_F))
+        def _():
+            stage_far(i - LAG_F, wave(i - LAG_F))
+
+    def steps_last(i):
+        @pl.when(i >= LAG_END)
+        def _():
+            zz = wave(i - LAG_END)
+            stage_last(i - LAG_END, zz)
+            multiply(zz)
+
+    def steps_first(i):
+        @pl.when(i < 6)
+        def _():
+            first(i + 2)
+
+    def steps_chain(i):
+        @pl.when(i < 6)
+        def _():
+            chain(i + 1, False)
+
+        for part in range(2):
+            @pl.when(i == 7 + part)
             def _():
-                z_copy(zz, 0).start()
-
-            for d in range(1, NX):
-                x_copy(zz, d).start()
-
-        @pl.when(i < NZ + LAG_Y)
-        def _():
-            zz = wave(i - LAG_Y)
-            for d in range(1, NX):
-                x_arrived(zz, up(x, d, NX)).wait_recv()
-            for way in range(2):
-                y_copy(zz, way).start()
-
-        @pl.when(jnp.logical_and(i >= LAG_F, i < NZ + LAG_F))
-        def _():
-            zz = wave(i - LAG_F)
-            for way in range(2):
-                y_arrived(zz, way).wait_recv()
-            for way in range(2):
-                f_copy(zz, way).start()
-
-        @pl.when(i < 6)
-        def _():
-            chain(i + 1, False)
-            first(i + 2)
-
+                chain_end(part)
+
+    def steps_row(i):
         @pl.when(i == 1)
         def _():
             first_copy(far(0)).wait_recv()
@@ -435,24 +503,32 @@
         def _():
             line(i - 1, False)
 
-        @pl.when(i == 7)
-        def _():
-            chain_end()
-
         @pl.when(i == 9)
         def _():
             line_end()
 
-        @pl.when(i == 3)
+    def steps_total(i):
+        @pl.when(i == TOTAL_AT)
+        def _():
+            @pl.loop(1, GROUPS)
+            def _(d):
+                total_copy(d).start()
+
+        @pl.when(i == TOTAL_AT + 3)
         def _():
             outer_results()
 
-        @pl.when(i >= LAG_END)
-        def _():
-            zz = wave(i - LAG_END)
-            for way in range(2):
-                f_arrived(zz, way).wait_recv()
-            multiply(zz)
+    steps = {
+        "near": steps_near, "line": steps_line, "far": steps_far, "last": steps_last,
+        "first": steps_first, "chain": steps_chain, "row": steps_row, "total": steps_total,
+    }
+    if LINE_EARLY:
+        stage_line(0, z)
+
+    @pl.loop(1, NZ + LAG_END)
+    def _(i):
+        for name in ORDER:
+            steps[name](i)
 
     keys_copy = remote(keys.at[tokens_of(other)], keys_in, pair_send.at[1], pair_recv.at[1], sibling)
     keys_copy.start()
@@ -477,11 +553,7 @@
             back_copy(zz, hi).wait_send()
             back_arrived(zz, hi).wait_recv()
         first_copy(zz).wait_send()
-        for d in range(1, NX):
-            x_copy(zz, d).wait_send()
-        for way in range(2):
-            y_copy(zz, way).wait_send()
-            f_copy(zz, way).wait_send()
+        stage_sent(zz, wave(zz))
 
     @pl.loop(0, 4)
     def _(d):
@@ -496,7 +568,8 @@
         coded_copy(d).wait_send()
         total_copy(d).wait_send()
         for way in range(2):
-            chain_copy(way, d - 1).wait_send()
+            for part in range(2):
+                chain_copy(way, d - 1, part).wait_send()
             line_copy(way, d - 1).wait_send()
 
 
@@ -575,8 +648,8 @@
             dma((NZ, 2)),
             dma((NZ, 2)),
             dma((NZ, 2)),
-            dma((2, 7)),
-            dma((2, 7)),
+            dma((2, 7, 2)),
+            dma((2, 7, 2)),
             dma((2,)),
             dma((2,)),
             dma((NZ,)),

time: 72.8 us -> 69 us (0.948)
  Pallas kernels: 72.1 us -> 67.8 us
    pallas_call x1, Pallas kernels: 69.5 us -> 65.2 us  [body(): pl.pallas_call(kernel, name='outer_step', out_shape=(pltpu.VMEM((rows, kw...]
where the time goes in v4:
time: 69 us; the launch traced here: 68.4 us
  Pallas kernels  67.8 us (98%)
    pallas_call x1, Pallas kernels, body(): pl.pallas_call(kernel, name='outer_step', out_shape=(pltpu.VMEM((rows, kw...  65.2 us
    pallas_call x1, Pallas kernels, body(): pl.pallas_call(finish, name='finish', out_shape=(jax.ShapeDtypeStruct((ro...  2.61 us

profile of v4, /device:TPU:1, one launch (start us, length us, event | category | flops | bytes accessed | tf_op | source)
XLA Modules:
  0.0 68.4 jit_solution(8517737761908203224)
XLA Ops:
  0.6 65.2 %outer_step.1 = (f32[256,512]{1,0:T(8,128)S(1)}, f32[256,512]{1,0:T(8,128)S(1)}, bf16[256,512]{1,0:T(8,128)(2,1)S(1)}, bf16[256,8192]{1,0:T(8,128)(2,1)S(1)}, f32[512,256]{1,0:T(8,128)S(1)}) custom-call(s32[256,512]{1,0:T(8,128)} %bitcast.2, f32[256,512]{1,0:T(8,128)} %master_hbm.1, f32[256,512]{1,0:T(8,128)} %momentum_hbm.1, bf16[256,8192]{1,0:T(8,128)(2,1)} %acts_hbm.1, ...), custom_call_target="tpu_custom_call" | custom-call | flops 6442450944 | bytes 16777216 | tf_op jit(solution)/shard_map/outer_step/pallas_call | solution.py:596
  65.8 2.6 %finish.1 = (f32[256,512]{1,0:T(8,128)}, f32[256,512]{1,0:T(8,128)}, bf16[256,512]{1,0:T(8,128)(2,1)}, bf16[256,8192]{1,0:T(8,128)(2,1)}, f32[256,512]{1,0:T(8,128)}) custom-call(f32[256,512]{1,0:T(8,128)S(1)} %get-tuple-element.15.weights, f32[256,512]{1,0:T(8,128)S(1)} %get-tuple-element.16.moved, bf16[256,512]{1,0:T(8,128)(2,1)S(1)} %get-tuple-element.17.keys, ...), custom_call_target="tpu_custom_call" | custom-call | tf_op jit(solution)/shard_map/finish/pallas_call | solution.py:669

commit v5 on v4

--- a/solution.py
+++ b/solution.py
@@ -14,9 +14,9 @@
 GROUPS = 8
 LAG_Y, LAG_F, LAG_END = 1, 3, 5
 LINE_EARLY = 0
-TOTAL_AT = 2
+TOTAL_AT = 6
 ORDER = ("near", "line", "total", "row", "far", "first", "last", "chain")
-CROSS_FIRST = 80
+CROSS_FIRST = 96
 TURNED = (4, 6)
 
 
@@ -74,6 +74,11 @@
     x = 2 * x_hi + x_lo
     other = 1 - c
     sibling = device(x, y, z, other)
+    along_z = [device(x, y, up(z, d, NZ), c) for d in (1, NZ - 1)]
+    along_x = [device(up(x, d, NX), y, z, c) for d in range(NX)]
+    along_y = [device(x, up(y, d, NY), z, c) for d in range(NY)]
+    pair_x = 2 * x_hi + 1 - x_lo
+    pair_y = [device(pair_x, up(y, d, NY), z, c) for d in range(NY)]
 
     def member(j):
         return device(2 * x_hi + lax.div(j, NY), lax.rem(j, NY), z, c)
@@ -88,6 +93,27 @@
 
     def tokens_of(core):
         return pl.ds(pl.multiple_of(core * tokens, tokens), tokens)
+
+    def act_load(zz, hi):
+        return pltpu.make_async_copy(
+            acts_hbm.at[:, columns(hi, zz, c)], acts.at[zz, hi, tokens_of(c)], acts_load.at[zz, hi]
+        )
+
+    def act_swap(zz, hi):
+        return remote(
+            acts_hbm.at[:, columns(hi, zz, other)], acts.at[zz, hi, tokens_of(c)],
+            acts_send.at[0], acts_recv.at[zz, hi], sibling,
+        )
+
+    def act_arrived(zz, hi):
+        return remote(
+            acts_hbm.at[:, columns(hi, zz, other)], acts.at[zz, hi, tokens_of(other)],
+            acts_send.at[0], acts_recv.at[zz, hi], sibling,
+        )
+
+    def far(i):
+        step = lax.div(i + 1, 2)
+        return lax.rem(z + 4 + step * (2 * lax.rem(i, 2) - 1) * -1 + NZ, NZ)
 
     loads = [
         pltpu.make_async_copy(delta_hbm, delta, load_sem.at[0]),
@@ -95,43 +121,16 @@
         pltpu.make_async_copy(master_hbm, master, load_sem.at[2]),
         pltpu.make_async_copy(momentum_hbm, momentum, load_sem.at[3]),
     ]
-    for load in loads:
-        load.start()
-
-    def act_load(zz, hi):
-        return pltpu.make_async_copy(
-            acts_hbm.at[:, columns(hi, zz, c)], acts.at[zz, hi, tokens_of(c)], acts_load.at[zz, hi]
-        )
-
-    def act_swap(zz, hi):
-        return remote(
-            acts_hbm.at[:, columns(hi, zz, other)], acts.at[zz, hi, tokens_of(c)],
-            acts_send.at[zz, hi], acts_recv.at[zz, hi], sibling,
-        )
-
-    def act_arrived(zz, hi):
-        return remote(
-            acts_hbm.at[:, columns(hi, zz, other)], acts.at[zz, hi, tokens_of(other)],
-            acts_send.at[zz, hi], acts_recv.at[zz, hi], sibling,
-        )
-
-    def far(i):
-        step = lax.div(i + 1, 2)
-        return lax.rem(z + 4 + step * (2 * lax.rem(i, 2) - 1) * -1 + NZ, NZ)
-
-    @pl.loop(0, NZ)
-    def _(i):
-        for hi in range(2):
-            act_load(far(i), hi).start()
-
-    partners = [sibling]
-    partners += [device(x, y, up(z, d, NZ), c) for d in (1, NZ - 1)]
-    partners += [device(up(x, d, NX), y, z, c) for d in range(1, NX)]
-    partners += [device(x, up(y, d, NY), z, c) for d in range(1, NY)]
-    partners += [device(2 * x_hi + 1 - x_lo, up(y, d, NY), z, c) for d in range(1, NY)]
+    loads[0].start()
+
+    partners = [sibling] + along_z + along_x[1:] + along_y[1:] + pair_y[1:]
     barrier = pltpu.get_barrier_semaphore()
     for partner in partners:
         pl.semaphore_signal(barrier, inc=1, device_id=partner, device_id_type=MESH)
+    for load in loads[1:]:
+        load.start()
+    for hi in range(2):
+        act_load(far(0), hi).start()
 
     loads[0].wait()
     for j in range(GROUPS):
@@ -144,7 +143,7 @@
 
     def coded_copy(d):
         j = up(g, d, GROUPS)
-        return remote(coded.at[j], coded_in.at[g], coded_send.at[d], coded_recv.at[g], member(j))
+        return remote(coded.at[j], coded_in.at[g], coded_send.at[0], coded_recv.at[g], member(j))
 
     def coded_arrived(j):
         return remote(coded.at[j], coded_in.at[j], coded_send.at[0], coded_recv.at[j], sibling)
@@ -153,15 +152,19 @@
     def _(d):
         coded_copy(d).start()
 
+    cot_t_swap = remote(cot_t.at[c], cot_t.at[c], pair_send.at[2], pair_recv.at[2], sibling)
+    cot_t_swap.start()
+
+    for hi in range(2):
+        act_swap(far(0), hi).start()
     cot_swap = remote(cot_hbm, cot.at[tokens_of(c)], pair_send.at[0], pair_recv.at[0], sibling)
     cot_swap.start()
-    cot_t_swap = remote(cot_t.at[c], cot_t.at[c], pair_send.at[2], pair_recv.at[2], sibling)
-    cot_t_swap.start()
-
-    @pl.loop(0, NZ)
+
+    @pl.loop(1, NZ)
     def _(i):
         for hi in range(2):
             act_swap(far(i), hi).start()
+            act_load(far(i), hi).start()
 
 
     def acts_ready(zz):
@@ -170,10 +173,9 @@
             act_arrived(zz, hi).wait_recv()
 
     def chain_copy(way, k, part):
-        to = device(x, y, up(z, 1 if way == 0 else NZ - 1, NZ), c)
         return remote(
             chain_out.at[way, k, part], chain_in.at[way, k, part],
-            chain_send.at[way, k, part], chain_recv.at[way, k, part], to,
+            chain_send.at[0], chain_recv.at[way, k, part], along_z[way],
         )
 
     def share(h, zz, hi):
@@ -184,7 +186,7 @@
 
     def first_copy(zz):
         return remote(
-            first_out.at[zz], first_in.at[zz], first_send.at[zz], first_recv.at[zz], device(up(x, 2, NX), y, z, c)
+            first_out.at[zz], first_in.at[zz], first_send.at[0], first_recv.at[zz], along_x[2]
         )
 
     def first(i):
@@ -194,8 +196,7 @@
         first_copy(zz).start()
 
     def line_copy(way, k):
-        to = device(x, y, up(z, 1 if way == 0 else NZ - 1, NZ), c)
-        return remote(line_out.at[way, k], line_in.at[way, k], line_send.at[way, k], line_recv.at[way, k], to)
+        return remote(line_out.at[way, k], line_in.at[way, k], line_send.at[0], line_recv.at[way, k], along_z[way])
 
     def line(k, opening):
         s = lax.div(k + 1, 2)
@@ -258,25 +259,24 @@
     gathered[z, y, x] = updated.astype(BF16)
 
     def z_copy(zz, way):
-        to = device(x, y, up(z, 1 if way == 0 else NZ - 1, NZ), c)
-        return remote(gathered.at[zz, y, x], gathered.at[zz, y, x], z_send.at[zz, way], z_recv.at[zz], to)
+        return remote(gathered.at[zz, y, x], gathered.at[zz, y, x], z_send.at[0], z_recv.at[zz], along_z[way])
 
     def z_arrived(zz):
-        return remote(gathered.at[zz, y, x], gathered.at[zz, y, x], z_send.at[zz, 0], z_recv.at[zz], sibling)
+        return remote(gathered.at[zz, y, x], gathered.at[zz, y, x], z_send.at[0], z_recv.at[zz], sibling)
 
     def near_copy(zz, d, turned):
-        to = device(x, up(y, d, NY), z, c) if turned else device(up(x, d, NX), y, z, c)
+        to = along_y[d] if turned else along_x[d]
         part = gathered.at[zz, y, x]
-        return remote(part, part, x_send.at[zz, d], x_recv.at[zz, y if turned else x], to)
+        return remote(part, part, x_send.at[0], x_recv.at[zz, y if turned else x], to)
 
     def near_arrived(zz, d, turned):
         at = up(y if turned else x, d, NX)
         part = gathered.at[zz, at, x] if turned else gathered.at[zz, y, at]
-        return remote(part, part, x_send.at[zz, 0], x_recv.at[zz, at], sibling)
+        return remote(part, part, x_send.at[0], x_recv.at[zz, at], sibling)
 
     def neighbour(way, turned):
         d = 1 if way == 0 else NX - 1
-        return device(up(x, d, NX), y, z, c) if turned else device(x, up(y, d, NY), z, c)
+        return along_x[d] if turned else along_y[d]
 
     def line_of(zz, d, turned):
         return gathered.at[zz, :, up(x, d, NX)] if turned else gathered.at[zz, up(y, d, NY)]
@@ -288,19 +288,19 @@
 
     def y_copy(zz, way, turned):
         part = line_of(zz, 0, turned)
-        return remote(part, part, y_send.at[zz, way], y_recv.at[zz, way], neighbour(way, turned))
+        return remote(part, part, y_send.at[0], y_recv.at[zz, way], neighbour(way, turned))
 
     def y_arrived(zz, way, turned):
         part = line_of(zz, 3 if way == 0 else 1, turned)
-        return remote(part, part, y_send.at[zz, way], y_recv.at[zz, way], sibling)
+        return remote(part, part, y_send.at[0], y_recv.at[zz, way], sibling)
 
     def f_copy(zz, way, turned):
         part = half_of(zz, 3 if way == 0 else 1, way, turned)
-        return remote(part, part, f_send.at[zz, way], f_recv.at[zz, way], neighbour(way, turned))
+        return remote(part, part, f_send.at[0], f_recv.at[zz, way], neighbour(way, turned))
 
     def f_arrived(zz, way, turned):
         part = half_of(zz, 2, way, turned)
-        return remote(part, part, f_send.at[zz, way], f_recv.at[zz, way], sibling)
+        return remote(part, part, f_send.at[0], f_recv.at[zz, way], sibling)
 
     def either(i, step):
         if isinstance(i, int):
@@ -344,27 +344,14 @@
 
         either(i, step)
 
-    def stage_sent(i, zz):
-        def step(turned):
-            for d in range(1, NX):
-                near_copy(zz, d, turned).wait_send()
-            for way in range(2):
-                y_copy(zz, way, turned).wait_send()
-                f_copy(zz, way, turned).wait_send()
-
-        either(i, step)
-
     for way in range(2):
         z_copy(z, way).start()
     stage_near(0, z)
 
-    def total_copy(d):
-        return remote(
-            total.at[g], total.at[g], total_send.at[d], total_recv.at[g], member(up(g, d, GROUPS))
-        )
-
-    def total_arrived(j):
-        return remote(total.at[j], total.at[j], total_send.at[0], total_recv.at[j], sibling)
+    def total_copy(j, to):
+        return remote(total.at[j], total.at[j], total_send.at[0], total_recv.at[j], to)
+
+    pair_g = up(g, NY, GROUPS)
 
     acts_ready(far(1))
     acts_ready(far(2))
@@ -384,30 +371,41 @@
 
     def back_copy(zz, hi):
         return remote(
-            back.at[zz, hi], grads.at[:, columns(hi, zz, c)], back_send.at[zz, hi], back_recv.at[zz, hi], sibling
+            back.at[zz, hi], grads.at[:, columns(hi, zz, c)], back_send.at[0], back_recv.at[0], sibling
         )
 
     def back_arrived(zz, hi):
         return remote(
-            back.at[zz, hi], grads.at[:, columns(hi, zz, other)], back_send.at[zz, hi], back_recv.at[zz, hi], sibling
+            back.at[zz, hi], grads.at[:, columns(hi, zz, other)], back_send.at[0], back_recv.at[0], sibling
         )
 
     def back_of(rows, w):
         product = lax.dot_general(rows, w, (((1,), (1,)), ((), ())), preferred_element_type=F32)
         return (product * out_scale).astype(BF16)
 
-    def multiply(zz):
+    keys_copy = remote(keys.at[tokens_of(other)], keys_in, pair_send.at[1], pair_recv.at[1], sibling)
+
+    def multiply(zz, last):
+        parts = [gathered[zz, :, xx].reshape(block // 2, kw) for xx in range(NX)]
+        w = jnp.concatenate(parts, axis=0)
+        both = jnp.concatenate([acts[zz, hi] for hi in range(2)], axis=1)
+        keys[...] += jnp.dot(both, w, preferred_element_type=F32)
+
+        @pl.when(last)
+        def _():
+            keys_copy.start()
+
         for hi in range(2):
-            lower = [gathered[zz, :, 2 * hi + lo].reshape(block // 2, kw) for lo in range(2)]
-            w = jnp.concatenate(lower, axis=0)
-            back[zz, hi] = back_of(cot[tokens_of(other), :], w)
+            half_w = jnp.concatenate(parts[2 * hi : 2 * hi + 2], axis=0)
+            back[zz, hi] = back_of(cot[tokens_of(other), :], half_w)
             back_copy(zz, hi).start()
-            grads[:, columns(hi, zz, c)] = back_of(cot[tokens_of(c), :], w)
-            keys[...] += jnp.dot(acts[zz, hi], w, preferred_element_type=F32)
+        for hi in range(2):
+            half_w = jnp.concatenate(parts[2 * hi : 2 * hi + 2], axis=0)
+            grads[:, columns(hi, zz, c)] = back_of(cot[tokens_of(c), :], half_w)
 
     def cross_copy(h):
         return remote(
-            cross_out.at[h], cross_in.at[h], cross_send.at[h], cross_recv.at[h], device(up(x, 2, NX), y, z, c)
+            cross_out.at[h], cross_in.at[h], cross_send.at[0], cross_recv.at[h], along_x[2]
         )
 
     def chain_end(part):
@@ -424,10 +422,10 @@
                 cross_copy(h).start()
 
     def outer_results():
-        for j in range(GROUPS):
-            @pl.when(g != j)
-            def _():
-                total_arrived(j).wait_recv()
+        @pl.loop(1, NY)
+        def _(d):
+            for lo in range(2):
+                total_copy(lo * NY + up(y, d, NY), sibling).wait_recv()
 
         for j in range(GROUPS):
             own = pl.ds(j * piece, piece)
@@ -465,7 +463,7 @@
         def _():
             zz = wave(i - LAG_END)
             stage_last(i - LAG_END, zz)
-            multiply(zz)
+            multiply(zz, i == NZ + LAG_END - 1)
 
     def steps_first(i):
         @pl.when(i < 6)
@@ -510,11 +508,16 @@
     def steps_total(i):
         @pl.when(i == TOTAL_AT)
         def _():
-            @pl.loop(1, GROUPS)
-            def _(d):
-                total_copy(d).start()
-
-        @pl.when(i == TOTAL_AT + 3)
+            total_copy(g, pair_y[0]).start()
+
+        @pl.when(i == TOTAL_AT + 1)
+        def _():
+            total_copy(pair_g, sibling).wait_recv()
+            for d in range(1, NY):
+                total_copy(g, along_y[d]).start()
+                total_copy(pair_g, along_y[d]).start()
+
+        @pl.when(i == TOTAL_AT + 4)
         def _():
             outer_results()
 
@@ -530,9 +533,6 @@
         for name in ORDER:
             steps[name](i)
 
-    keys_copy = remote(keys.at[tokens_of(other)], keys_in, pair_send.at[1], pair_recv.at[1], sibling)
-    keys_copy.start()
-
     for h in range(2):
         cross_copy(h).wait_recv()
         wgrad_out[pl.ds(h * half, late), :] = (cross_own[h] + cross_in[h].astype(F32)) * out_scale
@@ -543,34 +543,22 @@
     cot_swap.wait_send()
     cot_t_swap.wait_send()
     keys_copy.wait_send()
-    for h in range(2):
-        cross_copy(h).wait_send()
-
-    @pl.loop(0, NZ)
-    def _(zz):
-        for hi in range(2):
-            act_swap(zz, hi).wait_send()
-            back_copy(zz, hi).wait_send()
-            back_arrived(zz, hi).wait_recv()
-        first_copy(zz).wait_send()
-        stage_sent(zz, wave(zz))
-
-    @pl.loop(0, 4)
-    def _(d):
-        z_copy(up(z, d, NZ), 1).wait_send()
-
-    @pl.loop(0, 3)
-    def _(d):
-        z_copy(up(z, NZ - d, NZ), 0).wait_send()
-
-    @pl.loop(1, NZ)
-    def _(d):
-        coded_copy(d).wait_send()
-        total_copy(d).wait_send()
-        for way in range(2):
-            for part in range(2):
-                chain_copy(way, d - 1, part).wait_send()
-            line_copy(way, d - 1).wait_send()
+    for part, sem in (
+        (coded.at[pl.ds(0, 7)], coded_send),
+        (total.at[pl.ds(0, 7)], total_send),
+        (gathered.at[pl.ds(0, 7), 0, 0], z_send),
+        (gathered.at[pl.ds(0, 6), 0], x_send),
+        (gathered.at[pl.ds(0, 4)], y_send),
+        (gathered.at[pl.ds(0, 2)], f_send),
+        (chain_out, chain_send),
+        (line_out, line_send),
+        (first_out, first_send),
+        (cross_out, cross_send),
+        (back, acts_send),
+        (back, back_send),
+    ):
+        remote(part, part, sem.at[0], pair_recv.at[1], sibling).wait_send()
+    remote(back, back, back_send.at[0], back_recv.at[0], sibling).wait_recv()
 
 
 def finish(weights, moved, keys, grads, turned, weights_hbm, moved_hbm, keys_hbm, grads_hbm, wgrad_hbm, wgrad, sem):
@@ -632,32 +620,32 @@
             pltpu.VMEM((NZ, 2, tokens, block), BF16),
             dma((4,)),
             dma((NZ, 2)),
-            dma((NZ, 2)),
+            dma((1,)),
             dma((NZ, 2)),
             dma((3,)),
             dma((3,)),
+            dma((1,)),
             dma((GROUPS,)),
+            dma((1,)),
             dma((GROUPS,)),
-            dma((GROUPS,)),
-            dma((GROUPS,)),
+            dma((1,)),
+            dma((NZ,)),
+            dma((1,)),
+            dma((NZ, NX)),
+            dma((1,)),
             dma((NZ, 2)),
+            dma((1,)),
+            dma((NZ, 2)),
+            dma((1,)),
+            dma((2, 7, 2)),
+            dma((1,)),
+            dma((2,)),
+            dma((1,)),
             dma((NZ,)),
-            dma((NZ, NX)),
-            dma((NZ, NX)),
-            dma((NZ, 2)),
-            dma((NZ, 2)),
-            dma((NZ, 2)),
-            dma((NZ, 2)),
-            dma((2, 7, 2)),
-            dma((2, 7, 2)),
-            dma((2,)),
-            dma((2,)),
-            dma((NZ,)),
-            dma((NZ,)),
+            dma((1,)),
             dma((2, 7)),
-            dma((2, 7)),
-            dma((NZ, 2)),
-            dma((NZ, 2)),
+            dma((1,)),
+            dma((1,)),
         ],
         compiler_params=pltpu.CompilerParams(
             collective_id=0, has_side_effects=True, vmem_limit_bytes=44 * 2**20

time: 69 us -> 66.9 us (0.970)
  Pallas kernels: 67.8 us -> 66.2 us
    pallas_call x1, Pallas kernels: 65.2 us -> 63.6 us  [body(): pl.pallas_call(kernel, name='outer_step', out_shape=(pltpu.VMEM((rows, kw...]
where the time goes in v5:
time: 66.9 us; the launch traced here: 66.8 us
  Pallas kernels  66.2 us (99%)
    pallas_call x1, Pallas kernels, body(): pl.pallas_call(kernel, name='outer_step', out_shape=(pltpu.VMEM((rows, kw...  63.6 us
    pallas_call x1, Pallas kernels, body(): pl.pallas_call(finish, name='finish', out_shape=(jax.ShapeDtypeStruct((ro...  2.61 us

profile of v5, /device:TPU:1, one launch (start us, length us, event | category | flops | bytes accessed | tf_op | source)
XLA Modules:
  0.0 66.8 jit_solution(9126505383196129787)
XLA Ops:
  0.6 63.6 %outer_step.1 = (f32[256,512]{1,0:T(8,128)S(1)}, f32[256,512]{1,0:T(8,128)S(1)}, bf16[256,512]{1,0:T(8,128)(2,1)S(1)}, bf16[256,8192]{1,0:T(8,128)(2,1)S(1)}, f32[512,256]{1,0:T(8,128)S(1)}) custom-call(s32[256,512]{1,0:T(8,128)} %bitcast.2, f32[256,512]{1,0:T(8,128)} %master_hbm.1, f32[256,512]{1,0:T(8,128)} %momentum_hbm.1, bf16[256,8192]{1,0:T(8,128)(2,1)} %acts_hbm.1, ...), custom_call_target="tpu_custom_call" | custom-call | flops 6442450944 | bytes 16777216 | tf_op jit(solution)/shard_map/outer_step/pallas_call | solution.py:584
  64.2 2.6 %finish.1 = (f32[256,512]{1,0:T(8,128)}, f32[256,512]{1,0:T(8,128)}, bf16[256,512]{1,0:T(8,128)(2,1)}, bf16[256,8192]{1,0:T(8,128)(2,1)}, f32[256,512]{1,0:T(8,128)}) custom-call(f32[256,512]{1,0:T(8,128)S(1)} %get-tuple-element.15.weights, f32[256,512]{1,0:T(8,128)S(1)} %get-tuple-element.16.moved, bf16[256,512]{1,0:T(8,128)(2,1)S(1)} %get-tuple-element.17.keys, ...), custom_call_target="tpu_custom_call" | custom-call | tf_op jit(solution)/shard_map/finish/pallas_call | solution.py:657

commit v6 on v5

--- a/solution.py
+++ b/solution.py
@@ -14,7 +14,8 @@
 GROUPS = 8
 LAG_Y, LAG_F, LAG_END = 1, 3, 5
 LINE_EARLY = 0
-TOTAL_AT = 6
+TOTAL_AT, TOTAL_ON, TOTAL_END = 4, 7, 11
+NEAR_AT = (1, 1, 2, 2, 3, 3, 6)
 ORDER = ("near", "line", "total", "row", "far", "first", "last", "chain")
 CROSS_FIRST = 96
 TURNED = (4, 6)
@@ -137,8 +138,6 @@
         for k in range(kw // 128):
             codes = delta[pl.ds(j * piece, piece), pl.ds(k * 128, 128)]
             coded[j, :, pl.ds(k * 128, 128)] = dequantize(codes).astype(BF16)
-    loads[1].wait()
-    cot_t[c] = cot[tokens_of(c), :].T.reshape(2, half, tokens)
     pl.semaphore_wait(barrier, len(partners))
 
     def coded_copy(d):
@@ -152,11 +151,13 @@
     def _(d):
         coded_copy(d).start()
 
+    for hi in range(2):
+        act_swap(far(0), hi).start()
+    loads[1].wait()
+    cot_t[c] = cot[tokens_of(c), :].T.reshape(2, half, tokens)
     cot_t_swap = remote(cot_t.at[c], cot_t.at[c], pair_send.at[2], pair_recv.at[2], sibling)
     cot_t_swap.start()
 
-    for hi in range(2):
-        act_swap(far(0), hi).start()
     cot_swap = remote(cot_hbm, cot.at[tokens_of(c)], pair_send.at[0], pair_recv.at[0], sibling)
     cot_swap.start()
 
@@ -432,20 +433,15 @@
             weights_out[own, :], moved_out[own, :] = nesterov(total[j], master[own, :], momentum[own, :])
 
     def steps_near(i):
-        for j in (2 * i - 1, 2 * i):
-            @pl.when(j < NZ)
+        for j, at in enumerate(NEAR_AT, 1):
+            @pl.when(i == at)
             def _():
                 zz = wave(j)
                 z_arrived(zz).wait_recv()
-
-                @pl.when(jnp.logical_and(lax.rem(j, 2) == 1, j < 7))
-                def _():
+                if j % 2 == 1 and j < 7:
                     z_copy(zz, 1).start()
-
-                @pl.when(jnp.logical_and(lax.rem(j, 2) == 0, j < 6))
-                def _():
+                if j % 2 == 0 and j < 6:
                     z_copy(zz, 0).start()
-
                 stage_near(j, zz)
 
     def steps_line(i):
@@ -510,14 +506,14 @@
         def _():
             total_copy(g, pair_y[0]).start()
 
-        @pl.when(i == TOTAL_AT + 1)
+        @pl.when(i == TOTAL_ON)
         def _():
             total_copy(pair_g, sibling).wait_recv()
             for d in range(1, NY):
                 total_copy(g, along_y[d]).start()
                 total_copy(pair_g, along_y[d]).start()
 
-        @pl.when(i == TOTAL_AT + 4)
+        @pl.when(i == TOTAL_END)
         def _():
             outer_results()
 
@@ -562,12 +558,14 @@
 
 
 def finish(weights, moved, keys, grads, turned, weights_hbm, moved_hbm, keys_hbm, grads_hbm, wgrad_hbm, wgrad, sem):
-    pairs = ((grads, grads_hbm), (weights, weights_hbm), (moved, moved_hbm), (keys, keys_hbm), (wgrad, wgrad_hbm))
+    rows = grads.shape[0] // 4
+    pairs = [(grads.at[pl.ds(i * rows, rows)], grads_hbm.at[pl.ds(i * rows, rows)]) for i in range(4)]
+    pairs += [(weights, weights_hbm), (moved, moved_hbm), (keys, keys_hbm), (wgrad, wgrad_hbm)]
     copies = [pltpu.make_async_copy(src, dst, sem.at[i]) for i, (src, dst) in enumerate(pairs)]
-    for copy in copies[:4]:
+    for copy in copies[:-1]:
         copy.start()
     wgrad[...] = turned[...].T
-    copies[4].start()
+    copies[-1].start()
     for copy in copies:
         copy.wait()
 
@@ -666,7 +664,7 @@
         ),
         in_specs=[vmem] * 5,
         out_specs=(hbm,) * 5,
-        scratch_shapes=[pltpu.VMEM((rows, kw), F32), dma((5,))],
+        scratch_shapes=[pltpu.VMEM((rows, kw), F32), dma((8,))],
         compiler_params=pltpu.CompilerParams(vmem_limit_bytes=16 * 2**20),
     )(*[pltpu.with_memory_space_constraint(r, pltpu.VMEM) for r in results])
     return weights, moved, keys, grads, wgrad[None]

time: 66.9 us -> 66.6 us (level)
  no operation moved by 1% of the time
where the time goes in v6:
time: 66.6 us; the launch traced here: 66.5 us
  Pallas kernels  65.8 us (99%)
    pallas_call x1, Pallas kernels, body(): pl.pallas_call(kernel, name='outer_step', out_shape=(pltpu.VMEM((rows, kw...  63.2 us
    pallas_call x1, Pallas kernels, body(): pl.pallas_call(finish, name='finish', out_shape=(jax.ShapeDtypeStruct((ro...  2.64 us

profile of v6, /device:TPU:1, one launch (start us, length us, event | category | flops | bytes accessed | tf_op | source)
XLA Modules:
  0.0 66.5 jit_solution(5129920469664310021)
XLA Ops:
  0.6 63.2 %outer_step.1 = (f32[256,512]{1,0:T(8,128)S(1)}, f32[256,512]{1,0:T(8,128)S(1)}, bf16[256,512]{1,0:T(8,128)(2,1)S(1)}, bf16[256,8192]{1,0:T(8,128)(2,1)S(1)}, f32[512,256]{1,0:T(8,128)S(1)}) custom-call(s32[256,512]{1,0:T(8,128)} %bitcast.2, f32[256,512]{1,0:T(8,128)} %master_hbm.1, f32[256,512]{1,0:T(8,128)} %momentum_hbm.1, bf16[256,8192]{1,0:T(8,128)(2,1)} %acts_hbm.1, ...), custom_call_target="tpu_custom_call" | custom-call | flops 6442450944 | bytes 16777216 | tf_op jit(solution)/shard_map/outer_step/pallas_call | solution.py:582
  63.8 2.6 %finish.1 = (f32[256,512]{1,0:T(8,128)}, f32[256,512]{1,0:T(8,128)}, bf16[256,512]{1,0:T(8,128)(2,1)}, bf16[256,8192]{1,0:T(8,128)(2,1)}, f32[256,512]{1,0:T(8,128)}) custom-call(f32[256,512]{1,0:T(8,128)S(1)} %get-tuple-element.15.weights, f32[256,512]{1,0:T(8,128)S(1)} %get-tuple-element.16.moved, bf16[256,512]{1,0:T(8,128)(2,1)S(1)} %get-tuple-element.17.keys, ...), custom_call_target="tpu_custom_call" | custom-call | tf_op jit(solution)/shard_map/finish/pallas_call | solution.py:655

commit v7 on v6

--- a/solution.py
+++ b/solution.py
@@ -23,6 +23,20 @@
 
 def device(x, y, z, c):
     return (lax.rem(x, 2) * 4 + y, lax.div(x, 2) * 16 + z * 2 + c)
+
+
+def when(condition):
+    if isinstance(condition, bool):
+        return (lambda f: f()) if condition else (lambda f: None)
+    return pl.when(condition)
+
+
+def quotient(a, b):
+    return a // b if isinstance(a, int) else lax.div(a, b)
+
+
+def remainder(a, b):
+    return a % b if isinstance(a, int) else lax.rem(a, b)
 
 
 def up(v, d, n):
@@ -113,8 +127,8 @@
         )
 
     def far(i):
-        step = lax.div(i + 1, 2)
-        return lax.rem(z + 4 + step * (2 * lax.rem(i, 2) - 1) * -1 + NZ, NZ)
+        step = quotient(i + 1, 2)
+        return lax.rem(z + 4 + step * (1 - 2 * remainder(i, 2)) + NZ, NZ)
 
     loads = [
         pltpu.make_async_copy(delta_hbm, delta, load_sem.at[0]),
@@ -200,10 +214,10 @@
         return remote(line_out.at[way, k], line_in.at[way, k], line_send.at[0], line_recv.at[way, k], along_z[way])
 
     def line(k, opening):
-        s = lax.div(k + 1, 2)
+        s = quotient(k + 1, 2)
         for way in range(2):
             zz = up(z, 4 - s if way == 0 else 4 + s, NZ)
-            h = lax.rem(k + way, 2)
+            h = remainder(k + way, 2)
             if not opening:
                 line_copy(way, k - 2).wait_recv()
             sent = early_share(h, zz, x_hi) + first_in[zz, h].astype(F32)
@@ -223,11 +237,11 @@
             wgrad_out[pl.ds(h * half + late, CROSS_FIRST), :] = done * out_scale
 
     def chain(k, opening):
-        s = lax.div(k + 1, 2)
+        s = quotient(k + 1, 2)
         for part in range(2):
             for way in range(2):
                 zz = up(z, 4 - s if way == 0 else 4 + s, NZ)
-                h = lax.rem(k + way, 2)
+                h = remainder(k + way, 2)
                 sent = share(h, zz, x_hi if part else 1 - x_hi)
                 if not opening:
                     chain_copy(way, k - 2, part).wait_recv()
@@ -366,7 +380,7 @@
         acts_ready(far(i))
 
     def wave(i):
-        return lax.rem(z + lax.div(i + 1, 2) * (2 * lax.rem(i, 2) - 1) + NZ, NZ)
+        return lax.rem(z + quotient(i + 1, 2) * (2 * remainder(i, 2) - 1) + NZ, NZ)
 
     keys[...] = jnp.zeros_like(keys)
 
@@ -392,7 +406,7 @@
         both = jnp.concatenate([acts[zz, hi] for hi in range(2)], axis=1)
         keys[...] += jnp.dot(both, w, preferred_element_type=F32)
 
-        @pl.when(last)
+        @when(last)
         def _():
             keys_copy.start()
 
@@ -434,7 +448,7 @@
 
     def steps_near(i):
         for j, at in enumerate(NEAR_AT, 1):
-            @pl.when(i == at)
+            @when(i == at)
             def _():
                 zz = wave(j)
                 z_arrived(zz).wait_recv()
@@ -445,75 +459,75 @@
                 stage_near(j, zz)
 
     def steps_line(i):
-        @pl.when(jnp.logical_and(i >= LAG_Y + LINE_EARLY, i < NZ + LAG_Y))
+        @when(i >= LAG_Y + LINE_EARLY and i < NZ + LAG_Y)
         def _():
             stage_line(i - LAG_Y, wave(i - LAG_Y))
 
     def steps_far(i):
-        @pl.when(jnp.logical_and(i >= LAG_F, i < NZ + LAG_F))
+        @when(i >= LAG_F and i < NZ + LAG_F)
         def _():
             stage_far(i - LAG_F, wave(i - LAG_F))
 
     def steps_last(i):
-        @pl.when(i >= LAG_END)
+        @when(i >= LAG_END)
         def _():
             zz = wave(i - LAG_END)
             stage_last(i - LAG_END, zz)
             multiply(zz, i == NZ + LAG_END - 1)
 
     def steps_first(i):
-        @pl.when(i < 6)
+        @when(i < 6)
         def _():
             first(i + 2)
 
     def steps_chain(i):
-        @pl.when(i < 6)
+        @when(i < 6)
         def _():
             chain(i + 1, False)
 
         for part in range(2):
-            @pl.when(i == 7 + part)
+            @when(i == 7 + part)
             def _():
                 chain_end(part)
 
     def steps_row(i):
-        @pl.when(i == 1)
+        @when(i == 1)
         def _():
             first_copy(far(0)).wait_recv()
             line(0, True)
 
-        @pl.when(i == 2)
+        @when(i == 2)
         def _():
             first_copy(far(1)).wait_recv()
             first_copy(far(2)).wait_recv()
             line(1, True)
 
-        @pl.when(jnp.logical_or(i == 4, i == 6))
+        @when(i == 4 or i == 6)
         def _():
             first_copy(far(i - 1)).wait_recv()
             first_copy(far(i)).wait_recv()
 
-        @pl.when(jnp.logical_and(i >= 3, i < 8))
+        @when(i >= 3 and i < 8)
         def _():
             line(i - 1, False)
 
-        @pl.when(i == 9)
+        @when(i == 9)
         def _():
             line_end()
 
     def steps_total(i):
-        @pl.when(i == TOTAL_AT)
+        @when(i == TOTAL_AT)
         def _():
             total_copy(g, pair_y[0]).start()
 
-        @pl.when(i == TOTAL_ON)
+        @when(i == TOTAL_ON)
         def _():
             total_copy(pair_g, sibling).wait_recv()
             for d in range(1, NY):
                 total_copy(g, along_y[d]).start()
                 total_copy(pair_g, along_y[d]).start()
 
-        @pl.when(i == TOTAL_END)
+        @when(i == TOTAL_END)
         def _():
             outer_results()
 
@@ -524,8 +538,7 @@
     if LINE_EARLY:
         stage_line(0, z)
 
-    @pl.loop(1, NZ + LAG_END)
-    def _(i):
+    for i in range(1, NZ + LAG_END):
         for name in ORDER:
             steps[name](i)
 

time: 66.6 us -> 65.9 us (0.989)
  no operation moved by 1% of the time
where the time goes in v7:
time: 65.9 us; the launch traced here: 65.8 us
  Pallas kernels  65.2 us (99%)
    pallas_call x1, Pallas kernels, body(): pl.pallas_call(kernel, name='outer_step', out_shape=(pltpu.VMEM((rows, kw...  62.5 us
    pallas_call x1, Pallas kernels, body(): pl.pallas_call(finish, name='finish', out_shape=(jax.ShapeDtypeStruct((ro...  2.64 us

profile of v7, /device:TPU:1, one launch (start us, length us, event | category | flops | bytes accessed | tf_op | source)
XLA Modules:
  0.0 65.8 jit_solution(5009517325594150281)
XLA Ops:
  0.6 62.5 %outer_step.1 = (f32[256,512]{1,0:T(8,128)S(1)}, f32[256,512]{1,0:T(8,128)S(1)}, bf16[256,512]{1,0:T(8,128)(2,1)S(1)}, bf16[256,8192]{1,0:T(8,128)(2,1)S(1)}, f32[512,256]{1,0:T(8,128)S(1)}) custom-call(s32[256,512]{1,0:T(8,128)} %bitcast.2, f32[256,512]{1,0:T(8,128)} %master_hbm.1, f32[256,512]{1,0:T(8,128)} %momentum_hbm.1, bf16[256,8192]{1,0:T(8,128)(2,1)} %acts_hbm.1, ...), custom_call_target="tpu_custom_call" | custom-call | flops 6442450944 | bytes 16777216 | tf_op jit(solution)/shard_map/outer_step/pallas_call | solution.py:595
  63.2 2.6 %finish.1 = (f32[256,512]{1,0:T(8,128)}, f32[256,512]{1,0:T(8,128)}, bf16[256,512]{1,0:T(8,128)(2,1)}, bf16[256,8192]{1,0:T(8,128)(2,1)}, f32[256,512]{1,0:T(8,128)}) custom-call(f32[256,512]{1,0:T(8,128)S(1)} %get-tuple-element.15.weights, f32[256,512]{1,0:T(8,128)S(1)} %get-tuple-element.16.moved, bf16[256,512]{1,0:T(8,128)(2,1)S(1)} %get-tuple-element.17.keys, ...), custom_call_target="tpu_custom_call" | custom-call | tf_op jit(solution)/shard_map/finish/pallas_call | solution.py:668

commit v8 on v7

--- a/solution.py
+++ b/solution.py
@@ -13,7 +13,7 @@
 NX, NY, NZ = 4, 4, 8
 GROUPS = 8
 LAG_Y, LAG_F, LAG_END = 1, 3, 5
-LINE_EARLY = 0
+LINE_EARLY = 1
 TOTAL_AT, TOTAL_ON, TOTAL_END = 4, 7, 11
 NEAR_AT = (1, 1, 2, 2, 3, 3, 6)
 ORDER = ("near", "line", "total", "row", "far", "first", "last", "chain")
@@ -257,6 +257,8 @@
     acts_ready(far(0))
     chain(0, True)
     first(0)
+    acts_ready(far(1))
+    first(1)
 
     rows = pl.ds(pl.multiple_of(g * piece, piece), piece)
 
@@ -368,10 +370,8 @@
 
     pair_g = up(g, NY, GROUPS)
 
-    acts_ready(far(1))
     acts_ready(far(2))
     chain(1, True)
-    first(1)
     first(2)
     remote(cot_hbm, cot.at[tokens_of(other)], pair_send.at[0], pair_recv.at[0], sibling).wait_recv()
 

time: 65.9 us -> 66.4 us (level)
  no operation moved by 1% of the time
where the time goes in v8:
time: 66.4 us; the launch traced here: 66.3 us
  Pallas kernels  65.6 us (99%)
    pallas_call x1, Pallas kernels, body(): pl.pallas_call(kernel, name='outer_step', out_shape=(pltpu.VMEM((rows, kw...  63 us
    pallas_call x1, Pallas kernels, body(): pl.pallas_call(finish, name='finish', out_shape=(jax.ShapeDtypeStruct((ro...  2.64 us

profile of v8, /device:TPU:1, one launch (start us, length us, event | category | flops | bytes accessed | tf_op | source)
XLA Modules:
  0.0 66.3 jit_solution(8383257569992555885)
XLA Ops:
  0.6 63.0 %outer_step.1 = (f32[256,512]{1,0:T(8,128)S(1)}, f32[256,512]{1,0:T(8,128)S(1)}, bf16[256,512]{1,0:T(8,128)(2,1)S(1)}, bf16[256,8192]{1,0:T(8,128)(2,1)S(1)}, f32[512,256]{1,0:T(8,128)S(1)}) custom-call(s32[256,512]{1,0:T(8,128)} %bitcast.2, f32[256,512]{1,0:T(8,128)} %master_hbm.1, f32[256,512]{1,0:T(8,128)} %momentum_hbm.1, bf16[256,8192]{1,0:T(8,128)(2,1)} %acts_hbm.1, ...), custom_call_target="tpu_custom_call" | custom-call | flops 6442450944 | bytes 16777216 | tf_op jit(solution)/shard_map/outer_step/pallas_call | solution.py:595
  63.6 2.6 %finish.1 = (f32[256,512]{1,0:T(8,128)}, f32[256,512]{1,0:T(8,128)}, bf16[256,512]{1,0:T(8,128)(2,1)}, bf16[256,8192]{1,0:T(8,128)(2,1)}, f32[256,512]{1,0:T(8,128)}) custom-call(f32[256,512]{1,0:T(8,128)S(1)} %get-tuple-element.15.weights, f32[256,512]{1,0:T(8,128)S(1)} %get-tuple-element.16.moved, bf16[256,512]{1,0:T(8,128)(2,1)S(1)} %get-tuple-element.17.keys, ...), custom_call_target="tpu_custom_call" | custom-call | tf_op jit(solution)/shard_map/finish/pallas_call | solution.py:668
